TPU v7x, 32 devices: a whole 2x2x4 slice. The times are simulated.
32 devices in a mesh: lat: 4 (over x, core), lon: 8 (over z, y).
Axes of the slice: x: 2, y: 2, z: 4, core: 2. Of those that a mesh axis runs over, the one named last changes fastest.
Arguments:
- vorticity: float32 [16, 2, 256, 8192], P(None, None, 'lat', 'lon'), may hold values from -6 to 6
- legendre: bfloat16 [2048, 2048, 256], P(('lat', 'lon')), may hold values from -0.25 to 0.25
- wave_order: int32 [2048], replicated, may hold values from 0 to 2047, each once
Outputs:
- spectral: float32 [2048, 2, 16, 2048], P(('lat', 'lon'))
Inputs may be any that keep to these rules, and one draw needn't show every extreme that they name: wave_order is a permutation: every wavenumber below 2048 is held by exactly one slot.
All inputs are finite; a program needn't handle non-finite values.
Results may differ from a plain program's by a relative error of at most 0.0029.
Values may be sent and summed in bfloat16 or wider, within the bound.
No kernel may reach another device: no remote copies, remote signals or barrier semaphores. Data moves between devices by JAX's collectives and lax.ppermute only.
A program may use at most 192 MiB of HBM per device.

v0:
```python
import math

import jax
import jax.numpy as jnp
from jax import lax
from jax.sharding import PartitionSpec as P

MW = 2048


def angle_table(first_index, second_index, period):
    product = first_index[:, None] * second_index[None, :] % period
    return 2.0 * math.pi / period * product.astype(jnp.float32)


def fourier_rows(received):
    levels, hemis, items, circle = received.shape
    second_len = circle // 64
    kept_second = MW // 64
    flat_rows = received.reshape(levels * hemis * items, 64, second_len)
    index_first = jnp.arange(64, dtype=jnp.int32)
    index_second = jnp.arange(second_len, dtype=jnp.int32)
    index_kept = jnp.arange(kept_second, dtype=jnp.int32)
    angle_first = angle_table(index_first, index_first, 64)
    cos_first = jnp.cos(angle_first)
    sin_first = jnp.sin(angle_first)
    high = lax.Precision.HIGHEST
    first_real = jnp.einsum("rab,ak->rkb", flat_rows, cos_first, precision=high)
    first_imag = -jnp.einsum("rab,ak->rkb", flat_rows, sin_first, precision=high)
    angle_twist = (
        2.0
        * math.pi
        / circle
        * (index_first[:, None] * index_second[None, :] % circle).astype(jnp.float32)
    )
    twist_cos = jnp.cos(angle_twist)
    twist_sin = jnp.sin(angle_twist)
    middle_real = first_real * twist_cos + first_imag * twist_sin
    middle_imag = first_imag * twist_cos - first_real * twist_sin
    angle_second = angle_table(index_second, index_kept, second_len)
    cos_second = jnp.cos(angle_second)
    sin_second = jnp.sin(angle_second)
    final_real = jnp.einsum("rkb,bq->rqk", middle_real, cos_second, precision=high) + jnp.einsum(
        "rkb,bq->rqk", middle_imag, sin_second, precision=high
    )
    final_imag = jnp.einsum("rkb,bq->rqk", middle_imag, cos_second, precision=high) - jnp.einsum(
        "rkb,bq->rqk", middle_real, sin_second, precision=high
    )
    stacked = jnp.stack([final_real, final_imag], axis=1) * (1.0 / math.sqrt(circle))
    return stacked.reshape(levels, hemis, items, 2, MW).astype(jnp.bfloat16)


def combine_parts(product, parity, limit_rows, degree_cols, levels):
    count = product.shape[0]
    product = product.reshape(count, 2, 2, levels, product.shape[-1])
    combined = product[:, 0] + parity * product[:, 1]
    keep_mask = degree_cols[None, :] < limit_rows[:, None]
    return jnp.where(keep_mask[:, None, None, :], combined, jnp.zeros_like(combined))


def on_device(vorticity, legendre, wave_order):
    fourier = fourier_rows(
        lax.all_to_all(vorticity, "lon", split_axis=0, concat_axis=3, tiled=True)
    )
    chosen = jnp.take(fourier, wave_order, axis=4)
    packed = chosen[None, None]
    moved = lax.all_to_all(packed, ("lat", "lon"), split_axis=6, concat_axis=0, tiled=True)
    moved = moved.reshape((lax.axis_size("lat"), lax.axis_size("lon")) + moved.shape[2:])
    per_slot = jnp.transpose(moved, (6, 0, 4, 3, 5, 1, 2))
    slot_count = per_slot.shape[0]
    lat_total = per_slot.shape[1] * per_slot.shape[2]
    column_count = per_slot.shape[3] * per_slot.shape[4] * per_slot.shape[5] * per_slot.shape[6]
    levels = per_slot.shape[5] * per_slot.shape[6]
    per_slot = per_slot.reshape(slot_count, lat_total, column_count)
    wave_total = wave_order.shape[0]
    degree_count = legendre.shape[1]
    first_slot = lax.axis_index(("lat", "lon")) * slot_count
    local_waves = lax.dynamic_slice_in_dim(wave_order, first_slot, slot_count)
    limits = wave_total - local_waves
    degree_cols = jnp.arange(degree_count, dtype=jnp.int32)
    parity = (1 - 2 * (degree_cols % 2)).astype(jnp.float32)
    product = jnp.einsum("skj,sjq->sqk", legendre, per_slot, preferred_element_type=jnp.float32)
    return combine_parts(product, parity, limits, degree_cols, levels)


def solution(mesh):
    placed = (P(None, None, "lat", "lon"), P(("lat", "lon"), None, None), P())
    return jax.shard_map(
        on_device,
        mesh=mesh,
        in_specs=placed,
        out_specs=P(("lat", "lon"), None, None, None),
        check_vma=False,
    )
```

profile of v0, /device:TPU:0, one launch (start us, length us, event | category | flops | bytes accessed | tf_op | source)
XLA Modules:
  0.0 524.3 jit_solution(5531927048190070438)
XLA Ops:
  0.0 0.0 copy-start
  0.0 7.4 %all-to-all-start = ((f32[16,2,64,1024]{3,2,1,0:T(8,128)}), f32[16,2,64,1024]{3,2,1,0:T(8,128)}, u32[]{:S(2)}, u32[]{:S(2)}) async-start(f32[16,2,64,1024]{3,2,1,0:T(8,128)} %param.3), calls=%async_computation | async-start | bytes 16777216 | tf_op jit(solution)/shard_map/all_to_all | solution.py:63
  7.4 0.1 fusion.42
  7.6 0.0 copy-done
  7.6 183.0 %all-to-all-done = f32[16,2,64,1024]{3,2,1,0:T(8,128)} async-done(((f32[16,2,64,1024]{3,2,1,0:T(8,128)}), f32[16,2,64,1024]{3,2,1,0:T(8,128)}, u32[]{:S(2)}, u32[]{:S(2)}) %all-to-all-start) | async-done | bytes 8388640 | tf_op jit(solution)/shard_map/all_to_all | solution.py:63
  190.6 11.6 %copy.69 = f32[8,2,2,64,1024]{4,0,3,2,1:T(8,128)} copy(f32[8,2,2,64,1024]{4,3,2,1,0:T(8,128)} %bitcast.2) | data formatting | bytes 16777216 | tf_op jit(solution)/shard_map/all_to_all | solution.py:63
  202.2 9.3 %reshape.96 = f32[256,64,128]{2,1,0:T(8,128)} reshape(f32[2,2,64,8,1024]{4,3,2,1,0:T(8,128)} %bitcast.78) | data formatting | bytes 16777216 | tf_op jit(solution)/shard_map/reshape | solution.py:20
  211.5 11.9 %fusion.23 = f32[64,256,128]{2,0,1:T(8,128)} fusion(f32[256,64,128]{2,1,0:T(8,128)} %reshape.96), kind=kOutput, calls=%fused_computation.36 | convolution fusion | flops 1610670080 | bytes 16777216 | tf_op jit(solution)/shard_map/rab,ak->rkb/dot_general | solution.py:29
  223.4 14.0 %add_bitcast_fusion = (f32[256,64,128]{2,1,0:T(8,128)S(1)}, f32[256,64,128]{2,1,0:T(8,128)S(1)}) fusion(f32[64,256,128]{2,0,1:T(8,128)} %fusion.23, f32[64,128]{1,0:T(8,128)S(1)} %get-tuple-element.7, f32[64,128]{1,0:T(8,128)S(1)} %get-tuple-element.8, f32[256,64,128]{2,1,0:T(8,128)} %reshape.96), kind=kOutput, calls=%fused_computation.10 | convolution fusion | flops 1625350144 | bytes 33619968 | tf_op jit(solution)/shard_map/rab,ak->rkb/dot_general | solution.py:28
  237.4 11.8 %fusion.4 = f32[32,256,64]{1,0,2:T(8,128)S(1)} fusion(f32[256,64,128]{2,1,0:T(8,128)S(1)} %get-tuple-element.6), kind=kOutput, calls=%fused_computation.12 | convolution fusion | flops 805363712 | bytes 10485760 | tf_op jit(solution)/shard_map/rkb,bq->rqk/dot_general | solution.py:46
  249.2 20.5 %fusion.6 = f32[32,256,64]{1,0,2:T(8,128)S(1)} fusion(f32[256,64,128]{2,1,0:T(8,128)S(1)} %get-tuple-element.6), kind=kOutput, calls=%fused_computation.14 | convolution fusion | flops 805363712 | bytes 10485760 | tf_op jit(solution)/shard_map/rkb,bq->rqk/dot_general | solution.py:43
  269.8 13.4 %add_bitcast_fusion.1 = f32[256,32,64]{0,1,2:T(8,128)} fusion(f32[32,256,64]{1,0,2:T(8,128)S(1)} %fusion.6, f32[256,64,128]{2,1,0:T(8,128)S(1)} %get-tuple-element.5), kind=kOutput, calls=%fused_computation.22 | convolution fusion | flops 805888000 | bytes 12582912 | tf_op jit(solution)/shard_map/rkb,bq->rqk/dot_general | solution.py:43
  283.1 12.2 %subtract_bitcast_fusion.1 = f32[256,32,64]{0,1,2:T(8,128)S(1)} fusion(f32[32,256,64]{1,0,2:T(8,128)S(1)} %fusion.4, f32[256,64,128]{2,1,0:T(8,128)S(1)} %get-tuple-element.5), kind=kOutput, calls=%fused_computation.21 | convolution fusion | flops 805888000 | bytes 12582912 | tf_op jit(solution)/shard_map/rkb,bq->rqk/dot_general | solution.py:46
  295.4 4.5 copy.43
  299.9 3.6 stack.10
  303.5 6.9 %copy.45 = f32[2,2,64,1,2048]{2,3,4,1,0:T(1,128)} copy(f32[2,2,64,1,2048]{4,2,1,0,3:T(8,128)S(1)} %stack.10) | data formatting | bytes 4194304 | tf_op jit(solution)/shard_map/stack | solution.py:49
  310.4 5.6 %copy.40 = f32[256,32,64]{2,1,0:T(8,128)} copy(f32[256,32,64]{0,1,2:T(8,128)} %add_bitcast_fusion.1) | data formatting | bytes 4194304 | tf_op jit(solution)/shard_map/add | solution.py:43
  316.0 3.6 stack.9
  319.6 6.9 %copy.44 = f32[2,2,64,1,2048]{2,3,4,1,0:T(1,128)} copy(f32[2,2,64,1,2048]{4,2,1,0,3:T(8,128)S(1)} %stack.9) | data formatting | bytes 4194304 | tf_op jit(solution)/shard_map/stack | solution.py:49
  326.5 13.1 %fusion.3 = bf16[2,2,64,2,2048]{2,3,4,1,0:T(2,128)(2,1)} fusion(f32[2,2,64,1,2048]{2,3,4,1,0:T(1,128)} %copy.45, f32[2,2,64,1,2048]{2,3,4,1,0:T(1,128)} %copy.44), kind=kLoop, calls=%fused_computation.7 | loop fusion | flops 3145728 | bytes 6291456 | tf_op jit(solution)/shard_map/convert_element_type | solution.py:50
  339.6 26.0 %gather_fusion = bf16[2048,2,2,64,2]{3,4,2,1,0:T(2,128)(2,1)} fusion(bf16[2,2,64,2,2048]{2,3,4,1,0:T(2,128)(2,1)} %fusion.3, s32[2048]{0:T(1024)S(1)} %fusion.61), kind=kCustom, calls=%fused_computation | custom fusion | bytes 4202496 | tf_op jit(solution)/shard_map/jit(_take)/gather | solution.py:65
  365.6 9.3 %fusion.86 = bf16[2048,1,1,2,2,2,64]{6,5,4,3,2,1,0:T(2,128)(2,1)} fusion(bf16[2048,2,2,64,2]{3,4,2,1,0:T(2,128)(2,1)} %gather_fusion, pred[2048]{0:T(1024)(128)(4,1)S(1)} %compare_and_fusion), kind=kLoop, calls=%fused_computation.101 | loop fusion | flops 1048576 | bytes 4196352
  374.9 9.8 %reshape.113 = bf16[32,2,16384]{2,1,0:T(2,128)(2,1)} reshape(bf16[2048,1,1,2,2,2,64]{6,5,4,3,2,1,0:T(2,128)(2,1)} %fusion.86) | data formatting | bytes 4194304
  384.7 3.7 all-to-all-start.1
  388.4 0.1 dynamic-slice_subtract_fusion
  388.5 0.1 iota_compare_fusion
  388.6 49.8 %all-to-all-done.1 = bf16[32,2,16384]{2,1,0:T(2,128)(2,1)S(1)} async-done(((bf16[32,2,16384]{2,1,0:T(2,128)(2,1)}), bf16[32,2,16384]{2,1,0:T(2,128)(2,1)S(1)}, u32[]{:S(2)}, u32[]{:S(2)}) %all-to-all-start.1) | async-done | bytes 2097184 | tf_op jit(solution)/shard_map/all_to_all | solution.py:67
  438.5 4.0 reshape.114
  442.4 11.2 %copy.53 = bf16[1,1,2,2,64,2,32,64]{7,4,5,3,2,6,0,1:T(8,128)(2,1)} copy(bf16[1,1,2,2,64,2,32,64]{4,5,3,2,7,6,1,0:T(2,128)(2,1)} %bitcast.79) | data formatting | bytes 4194304 | tf_op jit(solution)/shard_map/all_to_all | solution.py:67
  453.6 9.3 %copy.49 = bf16[64,4,64,2,2,8,2]{2,1,6,5,4,3,0:T(4,128)(2,1)} copy(bf16[64,4,64,2,2,8,2]{0,2,4,3,6,5,1:T(8,128)(2,1)} %bitcast.80) | data formatting | bytes 4194304 | tf_op jit(solution)/shard_map/transpose | solution.py:69
  462.9 6.0 %reshape.98 = bf16[64,256,64]{1,2,0:T(8,128)(2,1)S(1)} reshape(bf16[64,4,64,2,2,8,2]{2,1,6,5,4,3,0:T(4,128)(2,1)} %copy.49) | data formatting | bytes 4194304 | tf_op jit(solution)/shard_map/reshape | solution.py:74
  468.9 37.5 %fusion.89 = f32[64,64,2048]{2,1,0:T(8,128)} fusion(bf16[64,256,64]{1,2,0:T(8,128)(2,1)S(1)} %reshape.98, bf16[64,2048,256]{2,1,0:T(8,128)(2,1)} %param.4), kind=kOutput, calls=%fused_computation.102 | convolution fusion | flops 4294967296 | bytes 102760448 | tf_op jit(solution)/shard_map/skj,sjq->sqk/dot_general | solution.py:82
  506.4 17.7 %fusion.2 = f32[64,2,16,2048]{3,2,1,0:T(8,128)} fusion(f32[64,2,2,16,2048]{4,3,2,1,0:T(8,128)} %bitcast.77, f32[2048]{0:T(1024)S(1)} %fusion.51, pred[64,2048]{1,0:T(8,128)(4,1)S(1)} %iota_compare_fusion), kind=kLoop, calls=%fused_computation.4 | loop fusion | flops 12582912 | bytes 50470912 | tf_op jit(solution)/shard_map/jit(_where)/select_n | solution.py:58
  (3 shorter events, 0.0 us)
Async XLA Ops:
  0.0 7.6 %copy-start = (s32[2048]{0:T(1024)S(1)}, s32[2048]{0:T(1024)}, u32[]{:S(2)}) copy-start(s32[2048]{0:T(1024)} %param.5) | copy-start | bytes 24580
  0.0 190.6 %all-to-all-start = ((f32[16,2,64,1024]{3,2,1,0:T(8,128)}), f32[16,2,64,1024]{3,2,1,0:T(8,128)}, u32[]{:S(2)}, u32[]{:S(2)}) async-start(f32[16,2,64,1024]{3,2,1,0:T(8,128)} %param.3), calls=%async_computation | async-start | bytes 16777216 | tf_op jit(solution)/shard_map/all_to_all | solution.py:63
  384.7 53.8 %all-to-all-start.1 = ((bf16[32,2,16384]{2,1,0:T(2,128)(2,1)}), bf16[32,2,16384]{2,1,0:T(2,128)(2,1)S(1)}, u32[]{:S(2)}, u32[]{:S(2)}) async-start(bf16[32,2,16384]{2,1,0:T(2,128)(2,1)} %reshape.113), calls=%async_computation.1 | async-start | bytes 4194304 | tf_op jit(solution)/shard_map/all_to_all | solution.py:67
where the time goes:
time: 534 us; the launch traced here: 524 us
  waiting for transfers between devices  233 us (44%)
  matrix products  121 us (23%)
  local copies, waits for them, and re-layouts  118 us (22%)
  other arithmetic  40.4 us (8%)
  starting transfers between devices  11.1 us (2%)
    all_to_all x1, waiting for transfers between devices, on_device(): lax.all_to_all(vorticity, 'lon', split_axis=0, concat_axis=3, tiled=True)  183 us
    all_to_all x1, waiting for transfers between devices, on_device(): lax.all_to_all(packed, ('lat', 'lon'), split_axis=6, concat_axis=0, tiled...  49.8 us
    dot_general x1, matrix products, on_device(): jnp.einsum('skj,sjq->sqk', legendre, per_slot, preferred_element_type=jnp...  37.5 us
    gather x1, local copies, waits for them, and re-layouts, on_device(): chosen = jnp.take(fourier, wave_order, axis=4)  26 us
    another operation x4, local copies, waits for them, and re-layouts, fourier_rows(): jnp.stack([final_real, final_imag], axis=1) * (1.0 / math.sqrt(circle))  21.1 us
    dot_general x1, matrix products, fourier_rows(): jnp.einsum('rkb,bq->rqk', middle_imag, sin_second, precision=high)  20.5 us
    select_n x1, other arithmetic, combine_parts(): jnp.where(keep_mask[:, None, None, :], combined, jnp.zeros_like(combined))  17.7 us
    dot_general x1, matrix products, fourier_rows(): first_real = jnp.einsum('rab,ak->rkb', flat_rows, cos_first, precision=high)  14 us
  transfers between devices with their start and end apart: 2, of which 2 were waited for; matrix products, arithmetic and copies ran while one was open for 0% of the time, Pallas kernels for 0%

commit v1 on v0

v1 whole, which is shorter than its diff:
```python
import functools
import math

import jax
import jax.numpy as jnp
import numpy as np
from jax import lax
from jax.experimental import pallas as pl
from jax.experimental.pallas import tpu as pltpu
from jax.sharding import PartitionSpec as P

MW = 2048
FIRST = 64
LANES = 128
KEEP = MW // FIRST
HALF = FIRST // 2 + 1
ROWS_K = 4 * KEEP
KTILE = 256
PRESCALE = 8192.0
VMEM = 56 * 1024 * 1024


def second_tables(circle):
    b = np.arange(LANES)[None, :]
    scale = 1.0 / math.sqrt(circle) / PRESCALE
    table = np.zeros((HALF, 2, KEEP, 2, 2 * LANES), np.float64)
    for k in range(HALF):
        for side in range(2):
            first = k if side == 0 else FIRST - k
            m = (first + FIRST * np.arange(KEEP))[:, None]
            angle = 2.0 * np.pi / circle * ((m * b) % circle)
            c, s = np.cos(angle), np.sin(angle)
            sign = 1.0 if side == 0 else -1.0
            table[k, side, :, 0, :LANES] = c
            table[k, side, :, 0, LANES:] = sign * s
            table[k, side, :, 1, :LANES] = -s
            table[k, side, :, 1, LANES:] = sign * c
    table = (table * scale).astype(np.float32).reshape(HALF, ROWS_K, 2 * LANES)
    high = table.astype(jnp.bfloat16)
    low = (table - high.astype(np.float32)).astype(jnp.bfloat16)
    return high, low


def add(a, b):
    return (a[0] + b[0], a[1] + b[1])


def sub(a, b):
    return (a[0] - b[0], a[1] - b[1])


def minus_i(a):
    return (a[1], -a[0])


def times(a, angle):
    c, s = math.cos(angle), math.sin(angle)
    return (a[0] * c + a[1] * s, a[1] * c - a[0] * s)


def real_dft8(x):
    r = math.sqrt(0.5)
    s04, d04 = x[0] + x[4], x[0] - x[4]
    s26, d26 = x[2] + x[6], x[2] - x[6]
    s15, d15 = x[1] + x[5], x[1] - x[5]
    s37, d37 = x[3] + x[7], x[3] - x[7]
    even, odd = s04 + s26, s15 + s37
    p, q = r * (d15 - d37), r * (d15 + d37)
    return [
        (even + odd, None),
        (d04 + p, -(d26 + q)),
        (s04 - s26, -(s15 - s37)),
        (d04 - p, d26 - q),
        (even - odd, None),
    ]


def complex_dft8(x):
    r = math.sqrt(0.5)

    def dft4(a, b, c, d):
        s, t, u, v = add(a, c), sub(a, c), add(b, d), minus_i(sub(b, d))
        return [add(s, u), add(t, v), sub(s, u), sub(t, v)]

    even = dft4(x[0], x[2], x[4], x[6])
    odd = dft4(x[1], x[3], x[5], x[7])
    o1 = ((odd[1][0] + odd[1][1]) * r, (odd[1][1] - odd[1][0]) * r)
    o2 = minus_i(odd[2])
    o3 = ((odd[3][1] - odd[3][0]) * r, -(odd[3][0] + odd[3][1]) * r)
    turned = [odd[0], o1, o2, o3]
    return [add(e, o) for e, o in zip(even, turned)] + [sub(e, o) for e, o in zip(even, turned)]


def fourier_kernel(rows, slots, index_ref, x_ref, high_ref, low_ref, out_ref, stage, y_high, y_low, full, picked):
    per_source = x_ref.shape[2] // LANES
    group = 16

    def put(k, row, value):
        for part in range(2):
            at = (k, pl.ds(row, group), pl.ds(part * LANES, LANES))
            v = value[part]
            if v is None:
                v = jnp.zeros((group, LANES), jnp.float32)
            h = v.astype(jnp.bfloat16)
            y_high[at] = h
            y_low[at] = (v - h.astype(jnp.float32)).astype(jnp.bfloat16)

    def first_step(step, carry):
        row = pl.multiple_of(step * group, group)
        for t in range(8):
            x = []
            for s in range(8):
                source, piece = divmod(8 * s + t, per_source)
                x.append(x_ref[source, pl.ds(row, group), pl.ds(piece * LANES, LANES)])
            for k1, (real, imag) in enumerate(real_dft8(x)):
                stage[t, k1, 0] = real
                if imag is not None:
                    stage[t, k1, 1] = imag
        for k2, value in enumerate(real_dft8([stage[t, 0, 0] for t in range(8)])):
            put(8 * k2, row, value)
        for k1 in range(1, 5):
            turned = []
            for t in range(8):
                angle = 2.0 * math.pi * t * k1 / FIRST
                if k1 == 4:
                    real = stage[t, k1, 0]
                    turned.append((real * math.cos(angle), real * -math.sin(angle)))
                else:
                    turned.append(times((stage[t, k1, 0], stage[t, k1, 1]), angle))
            for k2, value in enumerate(complex_dft8(turned)):
                k = k1 + 8 * k2
                if k < HALF:
                    put(k, row, value)
                elif k1 != 4:
                    put(FIRST - k, row, (value[0], -value[1]))
        return carry

    lax.fori_loop(0, rows // group, first_step, 0)

    def dot(a, b):
        return lax.dot_general(a, b, (((1,), (1,)), ((), ())), preferred_element_type=jnp.float32)

    def second_step(k, carry):
        at = pl.ds(pl.multiple_of(k * ROWS_K, ROWS_K), ROWS_K)
        full[at, :] = dot(high_ref[k], y_high[k]) + (dot(high_ref[k], y_low[k]) + dot(low_ref[k], y_high[k]))
        return carry

    lax.fori_loop(0, HALF, second_step, 0)

    def pick(step, carry):
        first = step * 8
        for i in range(8):
            at = pl.multiple_of(index_ref[first + i], 2)
            to = pl.multiple_of(step * 16, 16) + 2 * i
            picked[pl.ds(to, 2), :] = full[pl.ds(at, 2), :]
        return carry

    lax.fori_loop(0, slots // 8, pick, 0)
    out_ref[...] = picked[...].astype(jnp.bfloat16)


def fourier_slots(x, index, high, low):
    sources, rows, part = x.shape
    slots = index.shape[0]
    return pl.pallas_call(
        functools.partial(fourier_kernel, rows, slots),
        out_shape=jax.ShapeDtypeStruct((slots * 2, rows), jnp.bfloat16),
        in_specs=[pl.BlockSpec(memory_space=pltpu.SMEM)] + [pl.BlockSpec(memory_space=pltpu.VMEM)] * 3,
        out_specs=pl.BlockSpec(memory_space=pltpu.VMEM),
        scratch_shapes=[
            pltpu.VMEM((8, 5, 2, 16, LANES), jnp.float32),
            pltpu.VMEM((HALF, rows, 2 * LANES), jnp.bfloat16),
            pltpu.VMEM((HALF, rows, 2 * LANES), jnp.bfloat16),
            pltpu.VMEM((HALF * ROWS_K, rows), jnp.float32),
            pltpu.VMEM((slots * 2, rows), jnp.float32),
        ],
        compiler_params=pltpu.CompilerParams(vmem_limit_bytes=VMEM),
        cost_estimate=pl.CostEstimate(
            flops=6 * HALF * ROWS_K * rows * 2 * LANES, bytes_accessed=12 * 1024 * 1024, transcendentals=0
        ),
        name="fourier_slots",
    )(index, x, high, low)


def legendre_kernel(slots, tiles, buffers, limit_ref, data_ref, table_ref, out_ref, held, sems):
    slot = pl.program_id(0)
    degrees = tiles * KTILE

    def copy(s, tile):
        rows = pl.ds(tile * KTILE, KTILE)
        place = lax.rem(s, buffers)
        return pltpu.make_async_copy(table_ref.at[s, rows, :], held.at[place, rows, :], sems.at[place, tile])

    def start(s):
        for tile in range(tiles):

            @pl.when(tile * KTILE < limit_ref[s])
            def _():
                copy(s, tile).start()

    @pl.when(slot == 0)
    def _():
        for s in range(min(buffers - 1, slots)):
            start(s)

    @pl.when(slot + buffers - 1 < slots)
    def _():
        start(slot + buffers - 1)

    limit = limit_ref[slot]
    place = lax.rem(slot, buffers)
    data = data_ref[0]
    half = data.shape[0] // 2
    shape = out_ref.shape[1:3] + (KTILE,)
    degree = lax.broadcasted_iota(jnp.int32, (half, KTILE), 1)
    parity = (1 - 2 * (degree % 2)).astype(jnp.float32)
    for tile in range(tiles):
        cols = pl.ds(tile * KTILE, KTILE)

        @pl.when(tile * KTILE < limit)
        def _():
            copy(slot, tile).wait()
            product = lax.dot_general(
                data, held[place, cols, :], (((1,), (1,)), ((), ())), preferred_element_type=jnp.float32
            )
            both = product[:half] + parity * product[half:]
            both = jnp.where(degree < limit - tile * KTILE, both, 0.0)
            out_ref[0, :, :, cols] = both.reshape(shape)

        @pl.when(tile * KTILE >= limit)
        def _():
            out_ref[0, :, :, cols] = jnp.zeros(shape, jnp.float32)


def legendre_sum(limits, data, table, levels):
    slots, degrees, lats = table.shape
    columns = data.shape[1]
    tiles = degrees // KTILE
    buffers = 6
    return pl.pallas_call(
        functools.partial(legendre_kernel, slots, tiles, buffers),
        grid_spec=pltpu.PrefetchScalarGridSpec(
            num_scalar_prefetch=1,
            grid=(slots,),
            in_specs=[
                pl.BlockSpec((1, columns, lats), lambda s, lim: (s, 0, 0)),
                pl.BlockSpec(memory_space=pl.ANY),
            ],
            out_specs=pl.BlockSpec((1, 2, levels, degrees), lambda s, lim: (s, 0, 0, 0)),
            scratch_shapes=[
                pltpu.VMEM((buffers, degrees, lats), jnp.bfloat16),
                pltpu.SemaphoreType.DMA((buffers, tiles)),
            ],
        ),
        out_shape=jax.ShapeDtypeStruct((slots, 2, levels, degrees), jnp.float32),
        compiler_params=pltpu.CompilerParams(vmem_limit_bytes=VMEM),
        cost_estimate=pl.CostEstimate(
            flops=slots * degrees * lats * columns, bytes_accessed=slots * degrees * (lats + 64 * 2), transcendentals=0
        ),
        name="legendre_sum",
    )(limits, data, table)


def on_device(lat_size, lon_size, high, low, vorticity, legendre, wave_order):
    levels, hemis, lats, part = vorticity.shape
    slot_count = legendre.shape[0]
    waves = wave_order.astype(jnp.int32)
    lower, upper = waves % FIRST, waves // FIRST
    near = lower < HALF
    index = jnp.where(near, lower, FIRST - lower) * ROWS_K + jnp.where(near, 0, 2 * KEEP) + 2 * upper
    first_slot = lax.axis_index(("lat", "lon")) * slot_count
    limits = waves.shape[0] - lax.dynamic_slice_in_dim(waves, first_slot, slot_count)
    chunks = levels // lon_size
    pieces = []
    for chunk in range(chunks):
        block = vorticity[chunk * lon_size : (chunk + 1) * lon_size] * PRESCALE
        block = block.astype(jnp.float16).reshape(lon_size, hemis * lats, part)
        block = lax.all_to_all(block, "lon", split_axis=0, concat_axis=0, tiled=True)
        chosen = fourier_slots(block.astype(jnp.float32), index, high, low)
        chosen = chosen.reshape(lat_size * lon_size, slot_count * 2, hemis * lats)
        moved = lax.all_to_all(chosen, ("lat", "lon"), split_axis=0, concat_axis=0, tiled=True)
        moved = moved.reshape(lat_size, lon_size, slot_count, 2, hemis, lats)
        pieces.append(moved)
    data = jnp.stack(pieces, axis=0)
    data = jnp.transpose(data, (3, 5, 4, 0, 2, 1, 6)).reshape(slot_count, hemis * 2 * levels, lat_size * lats)
    return legendre_sum(limits, data, legendre, levels)


def solution(mesh):
    lat_size, lon_size = mesh.shape["lat"], mesh.shape["lon"]

    def whole(vorticity, legendre, wave_order):
        high, low = second_tables(vorticity.shape[3])
        body = functools.partial(on_device, lat_size, lon_size, high, low)
        return jax.shard_map(
            body,
            mesh=mesh,
            in_specs=(P(None, None, "lat", "lon"), P(("lat", "lon"), None, None), P()),
            out_specs=P(("lat", "lon"), None, None, None),
            check_vma=False,
        )(vorticity, legendre, wave_order)

    return whole
```

time: 534 us -> 277 us (0.52); the launches traced: 524 us -> 274 us
  waiting for transfers between devices: 233 us -> 57.5 us
  matrix products: 121 us -> 0 us
  Pallas kernels: 0 us -> 104 us
  local copies, waits for them, and re-layouts: 118 us -> 23.4 us
  blocking collectives: 0 us -> 55.5 us
  other arithmetic: 40.4 us -> 22.6 us
    all_to_all x2 -> x3, waiting for transfers between devices: 233 us -> 57.5 us  [the longest x2 31.2 us: on_device(): lax.all_to_all(chosen, ('lat', 'lon'), split_axis=0, concat_axis=0, tiled...]
    dot_general x7 -> x0, matrix products: 121 us -> none  [the longest x1 37.5 us: on_device(): jnp.einsum('skj,sjq->sqk', legendre, per_slot, preferred_element_type=jnp...]
    pallas_call x0 -> x3, Pallas kernels: none -> 104 us  [the longest x1 70.2 us: legendre_sum(): pl.pallas_call(functools.partial(legendre_kernel, slots, tiles, buffers),...]
    all_to_all x0 -> x1, blocking collectives: none -> 55.5 us  [on_device(): lax.all_to_all(block, 'lon', split_axis=0, concat_axis=0, tiled=True)]
    gather x1 -> x0, local copies, waits for them, and re-layouts: 26 us -> none  [on_device(): chosen = jnp.take(fourier, wave_order, axis=4)]
    all_to_all x2 -> x0, local copies, waits for them, and re-layouts: 22.8 us -> none  [the longest x1 11.6 us: on_device(): lax.all_to_all(vorticity, 'lon', split_axis=0, concat_axis=3, tiled=True)]
    select_n x1 -> x0, other arithmetic: 17.7 us -> none  [combine_parts(): jnp.where(keep_mask[:, None, None, :], combined, jnp.zeros_like(combined))]
    unnamed x4, local copies, waits for them, and re-layouts: 13.8 us -> 0.01 us
  transfers between devices with their start and end apart: 2 -> 3, of which waited for: 2 -> 3; matrix products, arithmetic and copies ran while one was open for 0% -> 4% of each run, Pallas kernels for 0% -> 12%
where the time goes in v1:
time: 277 us; the launch traced here: 274 us
  Pallas kernels  104 us (38%)
  waiting for transfers between devices  57.5 us (21%)
  blocking collectives  55.5 us (20%)
  local copies, waits for them, and re-layouts  23.4 us (8%)
  other arithmetic  22.6 us (8%)
  starting transfers between devices  10.6 us (4%)
    pallas_call x1, Pallas kernels, legendre_sum(): pl.pallas_call(functools.partial(legendre_kernel, slots, tiles, buffers),...  70.2 us
    all_to_all x1, blocking collectives, on_device(): lax.all_to_all(block, 'lon', split_axis=0, concat_axis=0, tiled=True)  55.5 us
    pallas_call x2, Pallas kernels, fourier_slots(): pl.pallas_call(functools.partial(fourier_kernel, rows, slots), out_shape=...  33.7 us
    all_to_all x2, waiting for transfers between devices, on_device(): lax.all_to_all(chosen, ('lat', 'lon'), split_axis=0, concat_axis=0, tiled...  31.2 us
    all_to_all x1, waiting for transfers between devices, on_device(): lax.all_to_all(block, 'lon', split_axis=0, concat_axis=0, tiled=True)  26.3 us
    another operation x2, local copies, waits for them, and re-layouts, on_device(): data = jnp.stack(pieces, axis=0)  8.84 us
    transpose x1, other arithmetic, on_device(): jnp.transpose(data, (3, 5, 4, 0, 2, 1, 6))  8.6 us
    transpose x1, local copies, waits for them, and re-layouts, on_device(): jnp.transpose(data, (3, 5, 4, 0, 2, 1, 6))  7.63 us
  transfers between devices with their start and end apart: 3, of which 3 were waited for; matrix products, arithmetic and copies ran while one was open for 4% of the time, Pallas kernels for 12%

profile of v1, /device:TPU:0, one launch (start us, length us, event | category | flops | bytes accessed | tf_op | source)
XLA Modules:
  0.0 273.8 jit_solution(4853444095527936352)
XLA Ops:
  0.0 6.1 %multiply_convert_fusion.1 = (f16[8,2,64,1024]{3,2,1,0:T(8,128)(2,1)S(1)}, f16[8,2,64,1024]{3,2,1,0:T(8,128)(2,1)}) fusion(f32[16,2,64,1024]{3,2,1,0:T(8,128)} %param.5), kind=kLoop, calls=%fused_computation.2 | loop fusion | flops 4194304 | bytes 12582912 | tf_op jit(solution)/shard_map/convert_element_type | solution.py:277
  6.1 0.0 copy-start.1
  6.1 55.5 %all_to_all.20 = f16[8,128,1024]{2,1,0:T(8,128)(2,1)} all-to-all(f16[8,128,1024]{2,1,0:T(8,128)(2,1)S(1)} %bitcast.7), channel_id=1, replica_groups=mesh['lat'=4,'lon'=8] {'lon'}, dimensions={0} | all-to-all | bytes 4194304 | tf_op jit(solution)/shard_map/all_to_all | solution.py:278
  61.6 3.6 %all-to-all-start.2 = ((f16[8,128,1024]{2,1,0:T(8,128)(2,1)}), f16[8,128,1024]{2,1,0:T(8,128)(2,1)S(1)}, u32[]{:S(2)}, u32[]{:S(2)}) async-start(f16[8,128,1024]{2,1,0:T(8,128)(2,1)} %bitcast.6), calls=%async_computation.2 | async-start | bytes 4194304 | tf_op jit(solution)/shard_map/all_to_all | solution.py:278
  65.2 0.0 copy-done.1
  65.3 0.6 fusion.1.index_ref
  65.9 4.1 %convert_element_type.13.x_ref = f32[8,128,1024]{2,1,0:T(8,128)} convert(f16[8,128,1024]{2,1,0:T(8,128)(2,1)} %all_to_all.20) | non-fusion elementwise | flops 1048576 | bytes 6291456 | tf_op jit(solution)/shard_map/convert_element_type | solution.py:279
  70.0 16.9 %fourier_slots.2 = bf16[4096,128]{1,0:T(8,128)(2,1)} custom-call(s32[2048]{0:T(1024)} %fusion.1.index_ref, f32[8,128,1024]{2,1,0:T(8,128)} %convert_element_type.13.x_ref, bf16[33,128,256]{2,1,0:T(8,128)(2,1)} %constant.55.clone.high_ref, bf16[33,128,256]{2,1,0:T(8,128)(2,1)} %constant.56.clone.low_ref), custom_call_target="tpu_custom_call" | custom-call | flops 830472192 | bytes 12582912 | tf_op jit(solution)/shard_map/fourier_slots/pallas_call | solution.py:165
  86.8 26.3 %all-to-all-done.2 = f16[8,128,1024]{2,1,0:T(8,128)(2,1)S(1)} async-done(((f16[8,128,1024]{2,1,0:T(8,128)(2,1)}), f16[8,128,1024]{2,1,0:T(8,128)(2,1)S(1)}, u32[]{:S(2)}, u32[]{:S(2)}) %all-to-all-start.2) | async-done | bytes 2097184 | tf_op jit(solution)/shard_map/all_to_all | solution.py:278
  113.1 3.7 %all-to-all-start.1 = ((bf16[32,128,128]{2,1,0:T(8,128)(2,1)}), bf16[32,128,128]{2,1,0:T(8,128)(2,1)S(1)}, u32[]{:S(2)}, u32[]{:S(2)}) async-start(bf16[32,128,128]{2,1,0:T(8,128)(2,1)} %bitcast.9), calls=%async_computation.1 | async-start | bytes 2097152 | tf_op jit(solution)/shard_map/all_to_all | solution.py:281
  116.8 2.5 convert_element_type.15.x_ref
  119.3 16.9 %fourier_slots.3 = bf16[4096,128]{1,0:T(8,128)(2,1)} custom-call(s32[2048]{0:T(1024)} %fusion.1.index_ref, f32[8,128,1024]{2,1,0:T(8,128)} %convert_element_type.15.x_ref, bf16[33,128,256]{2,1,0:T(8,128)(2,1)} %constant.55.clone.high_ref, bf16[33,128,256]{2,1,0:T(8,128)(2,1)} %constant.56.clone.low_ref), custom_call_target="tpu_custom_call" | custom-call | flops 830472192 | bytes 12582912 | tf_op jit(solution)/shard_map/fourier_slots/pallas_call | solution.py:165
  136.1 8.2 %all-to-all-done.1 = bf16[32,128,128]{2,1,0:T(8,128)(2,1)S(1)} async-done(((bf16[32,128,128]{2,1,0:T(8,128)(2,1)}), bf16[32,128,128]{2,1,0:T(8,128)(2,1)S(1)}, u32[]{:S(2)}, u32[]{:S(2)}) %all-to-all-start.1) | async-done | bytes 1048608 | tf_op jit(solution)/shard_map/all_to_all | solution.py:281
  144.4 0.0 copy-start
  144.4 3.4 %all-to-all-start.3 = ((bf16[32,128,128]{2,1,0:T(8,128)(2,1)}), bf16[32,128,128]{2,1,0:T(8,128)(2,1)}, u32[]{:S(2)}, u32[]{:S(2)}) async-start(bf16[32,128,128]{2,1,0:T(8,128)(2,1)} %bitcast.8), calls=%async_computation.3 | async-start | bytes 2097152 | tf_op jit(solution)/shard_map/all_to_all | solution.py:281
  147.8 0.0 copy-done
  147.8 0.7 dynamic-slice_subtract_fusion.limit_ref
  148.4 3.9 %stack_reshape.6 = bf16[1,4,8,64,2,2,64]{6,5,4,3,2,1,0:T(2,128)(2,1)S(1)} reshape(bf16[32,128,128]{2,1,0:T(8,128)(2,1)} %copy-done) | data formatting | bytes 2097152 | tf_op jit(solution)/shard_map/stack;reshape | solution.py:284
  152.3 23.0 %all-to-all-done.3 = bf16[32,128,128]{2,1,0:T(8,128)(2,1)} async-done(((bf16[32,128,128]{2,1,0:T(8,128)(2,1)}), bf16[32,128,128]{2,1,0:T(8,128)(2,1)}, u32[]{:S(2)}, u32[]{:S(2)}) %all-to-all-start.3) | async-done | bytes 1048608 | tf_op jit(solution)/shard_map/all_to_all | solution.py:281
  175.3 5.0 %stack_reshape.7 = bf16[1,4,8,64,2,2,64]{6,5,4,3,2,1,0:T(2,128)(2,1)} reshape(bf16[32,128,128]{2,1,0:T(8,128)(2,1)} %all-to-all-done.3) | data formatting | bytes 2097152 | tf_op jit(solution)/shard_map/stack;reshape | solution.py:284
  180.3 8.6 %maximum_bitcast_fusion = bf16[64,2,2,2,8,4,64]{6,1,2,0,4,5,3:T(2,128)(2,1)S(1)} fusion(bf16[1,4,8,64,2,2,64]{6,5,4,3,2,1,0:T(2,128)(2,1)} %stack_reshape.7, bf16[1,4,8,64,2,2,64]{6,5,4,3,2,1,0:T(2,128)(2,1)S(1)} %stack_reshape.6), kind=kLoop, calls=%fused_computation | loop fusion | flops 1048576 | bytes 4194304 | tf_op jit(solution)/shard_map/transpose | solution.py:285
  188.9 7.6 %copy.6 = bf16[64,2,2,2,8,4,64]{6,5,4,3,2,1,0:T(4,128)(2,1)} copy(bf16[64,2,2,2,8,4,64]{6,1,2,0,4,5,3:T(2,128)(2,1)S(1)} %maximum_bitcast_fusion) | data formatting | bytes 4194304 | tf_op jit(solution)/shard_map/transpose | solution.py:285
  196.5 7.0 %reshape.19.data_ref = bf16[64,64,256]{2,1,0:T(8,128)(2,1)} reshape(bf16[64,2,2,2,8,4,64]{6,5,4,3,2,1,0:T(4,128)(2,1)} %copy.6) | data formatting | bytes 4194304 | tf_op jit(solution)/shard_map/reshape | solution.py:285
  203.5 70.2 %legendre_sum.1 = f32[64,2,16,2048]{3,2,1,0:T(8,128)} custom-call(s32[64]{0:T(128)} %dynamic-slice_subtract_fusion.limit_ref, bf16[64,64,256]{2,1,0:T(8,128)(2,1)} %reshape.19.data_ref, bf16[64,2048,256]{2,1,0:T(8,128)(2,1)} %table_ref.1), custom_call_target="tpu_custom_call" | custom-call | flops 2147483648 | bytes 50331648 | tf_op jit(solution)/shard_map/legendre_sum/pallas_call | solution.py:240
Async XLA Ops:
  6.1 59.2 %copy-start.1 = (s32[2048]{0:T(1024)S(1)}, s32[2048]{0:T(1024)}, u32[]{:S(2)}) copy-start(s32[2048]{0:T(1024)} %param.7) | copy-start | bytes 24580
  61.6 51.5 %all-to-all-start.2 = ((f16[8,128,1024]{2,1,0:T(8,128)(2,1)}), f16[8,128,1024]{2,1,0:T(8,128)(2,1)S(1)}, u32[]{:S(2)}, u32[]{:S(2)}) async-start(f16[8,128,1024]{2,1,0:T(8,128)(2,1)} %bitcast.6), calls=%async_computation.2 | async-start | bytes 4194304 | tf_op jit(solution)/shard_map/all_to_all | solution.py:278
  113.1 31.2 %all-to-all-start.1 = ((bf16[32,128,128]{2,1,0:T(8,128)(2,1)}), bf16[32,128,128]{2,1,0:T(8,128)(2,1)S(1)}, u32[]{:S(2)}, u32[]{:S(2)}) async-start(bf16[32,128,128]{2,1,0:T(8,128)(2,1)} %bitcast.9), calls=%async_computation.1 | async-start | bytes 2097152 | tf_op jit(solution)/shard_map/all_to_all | solution.py:281
  144.4 3.4 %copy-start = (bf16[32,128,128]{2,1,0:T(8,128)(2,1)}, bf16[32,128,128]{2,1,0:T(8,128)(2,1)S(1)}, u32[]{:S(2)}) copy-start(bf16[32,128,128]{2,1,0:T(8,128)(2,1)S(1)} %all-to-all-done.1) | copy-start | bytes 3145732
  144.4 31.0 %all-to-all-start.3 = ((bf16[32,128,128]{2,1,0:T(8,128)(2,1)}), bf16[32,128,128]{2,1,0:T(8,128)(2,1)}, u32[]{:S(2)}, u32[]{:S(2)}) async-start(bf16[32,128,128]{2,1,0:T(8,128)(2,1)} %bitcast.8), calls=%async_computation.3 | async-start | bytes 2097152 | tf_op jit(solution)/shard_map/all_to_all | solution.py:281

commit v2 on v1

--- a/solution.py
+++ b/solution.py
@@ -91,7 +91,10 @@
     return [add(e, o) for e, o in zip(even, turned)] + [sub(e, o) for e, o in zip(even, turned)]
 
 
-def fourier_kernel(rows, slots, index_ref, x_ref, high_ref, low_ref, out_ref, stage, y_high, y_low, full, picked):
+def fourier_kernel(rows, slots, parts, index_ref, me_ref, x_ref, high_ref, low_ref, *refs):
+    out_refs = refs[:parts]
+    stage, y_high, y_low, full, picked = refs[parts:]
+    me = me_ref[0]
     per_source = x_ref.shape[2] // LANES
     group = 16
 
@@ -111,7 +114,7 @@
             x = []
             for s in range(8):
                 source, piece = divmod(8 * s + t, per_source)
-                x.append(x_ref[source, pl.ds(row, group), pl.ds(piece * LANES, LANES)])
+                x.append(x_ref[me ^ source, pl.ds(row, group), pl.ds(piece * LANES, LANES)])
             for k1, (real, imag) in enumerate(real_dft8(x)):
                 stage[t, k1, 0] = real
                 if imag is not None:
@@ -156,17 +159,20 @@
         return carry
 
     lax.fori_loop(0, slots // 8, pick, 0)
-    out_ref[...] = picked[...].astype(jnp.bfloat16)
-
-
-def fourier_slots(x, index, high, low):
+    length = slots * 2 // parts
+    for part in range(parts):
+        out_refs[part][...] = picked[pl.ds(part * length, length), :].astype(jnp.bfloat16)
+
+
+def fourier_slots(x, me, index, high, low, parts):
     sources, rows, part = x.shape
     slots = index.shape[0]
+    smem, vmem = pl.BlockSpec(memory_space=pltpu.SMEM), pl.BlockSpec(memory_space=pltpu.VMEM)
     return pl.pallas_call(
-        functools.partial(fourier_kernel, rows, slots),
-        out_shape=jax.ShapeDtypeStruct((slots * 2, rows), jnp.bfloat16),
-        in_specs=[pl.BlockSpec(memory_space=pltpu.SMEM)] + [pl.BlockSpec(memory_space=pltpu.VMEM)] * 3,
-        out_specs=pl.BlockSpec(memory_space=pltpu.VMEM),
+        functools.partial(fourier_kernel, rows, slots, parts),
+        out_shape=[jax.ShapeDtypeStruct((slots * 2 // parts, rows), jnp.bfloat16)] * parts,
+        in_specs=[smem, smem, vmem, vmem, vmem],
+        out_specs=[vmem] * parts,
         scratch_shapes=[
             pltpu.VMEM((8, 5, 2, 16, LANES), jnp.float32),
             pltpu.VMEM((HALF, rows, 2 * LANES), jnp.bfloat16),
@@ -179,111 +185,228 @@
             flops=6 * HALF * ROWS_K * rows * 2 * LANES, bytes_accessed=12 * 1024 * 1024, transcendentals=0
         ),
         name="fourier_slots",
-    )(index, x, high, low)
-
-
-def legendre_kernel(slots, tiles, buffers, limit_ref, data_ref, table_ref, out_ref, held, sems):
-    slot = pl.program_id(0)
-    degrees = tiles * KTILE
-
-    def copy(s, tile):
-        rows = pl.ds(tile * KTILE, KTILE)
-        place = lax.rem(s, buffers)
-        return pltpu.make_async_copy(table_ref.at[s, rows, :], held.at[place, rows, :], sems.at[place, tile])
-
-    def start(s):
-        for tile in range(tiles):
-
-            @pl.when(tile * KTILE < limit_ref[s])
+    )(index, me, x, high, low)
+
+
+def arrange_kernel(lat_size, lon_size, slots, moved_ref, out_ref, sorted_rows):
+    rows = slots * 2
+    for lat in range(lat_size):
+        for lon in range(lon_size):
+            block = moved_ref[lat * lon_size + lon].astype(jnp.float32)
+            sorted_rows[lat, pl.ds(lon, rows, stride=lon_size), :] = block
+    shape = (slots, 2 * lon_size, LANES)
+    lane = lax.broadcasted_iota(jnp.int32, (rows * lon_size, LANES), 1)
+    lower = lane < LANES // 2
+    for pair in range(lat_size // 2):
+        first, second = sorted_rows[2 * pair], sorted_rows[2 * pair + 1]
+        north = jnp.where(lower, first, pltpu.roll(second, LANES // 2, 1))
+        south = jnp.where(lower, pltpu.roll(first, LANES // 2, 1), second)
+        lanes = pl.ds(pair * LANES, LANES)
+        out_ref[:, 0, :, lanes] = north.reshape(shape).astype(jnp.bfloat16)
+        out_ref[:, 1, :, lanes] = south.reshape(shape).astype(jnp.bfloat16)
+
+
+def arrange(moved, lat_size, lon_size, slots):
+    rows = moved.shape[2]
+    lats = rows // 2
+    if rows != LANES or lon_size != 8:
+        moved = moved.reshape(lat_size, lon_size, slots, 2, 2, lats)
+        moved = jnp.transpose(moved, (2, 4, 3, 1, 0, 5))
+        return moved.reshape(slots, 2, 2 * lon_size, lat_size * lats)
+    return pl.pallas_call(
+        functools.partial(arrange_kernel, lat_size, lon_size, slots),
+        out_shape=jax.ShapeDtypeStruct((slots, 2, 2 * lon_size, lat_size * lats), jnp.bfloat16),
+        in_specs=[pl.BlockSpec(memory_space=pltpu.VMEM)],
+        out_specs=pl.BlockSpec(memory_space=pltpu.VMEM),
+        scratch_shapes=[pltpu.VMEM((lat_size, slots * 2 * lon_size, LANES), jnp.float32)],
+        compiler_params=pltpu.CompilerParams(vmem_limit_bytes=VMEM),
+        cost_estimate=pl.CostEstimate(flops=1024, bytes_accessed=16 * 1024 * 1024, transcendentals=0),
+        name="arrange",
+    )(moved)
+
+
+def legendre_kernel(begin, end, tiles, bases, first, *refs):
+    limit_ref, refs = refs[0], refs[1:]
+    data_refs, refs = refs[: len(bases)], refs[len(bases) :]
+    table_ref, refs = refs[0], refs[1 if first else 2 :]
+    out_ref, held, staged, in_sems, out_sems = refs
+    buffers, stages = held.shape[0], staged.shape[0]
+    levels = out_ref.shape[2]
+    part = levels // len(bases)
+    half = 2 * levels
+
+    def tile_count(slot):
+        return lax.div(limit_ref[slot] + (KTILE - 1), KTILE)
+
+    def fetch(slot, count):
+        place = lax.rem(slot, buffers)
+        rows = pl.ds(0, count * KTILE)
+        return pltpu.make_async_copy(table_ref.at[slot, rows, :], held.at[place, rows, :], in_sems.at[place])
+
+    def put(slot):
+        place = lax.rem(slot, stages)
+        return pltpu.make_async_copy(staged.at[place], out_ref.at[slot], out_sems.at[place])
+
+    def start(slot):
+        count = tile_count(slot)
+        for n in range(1, tiles + 1):
+
+            @pl.when(count == n)
             def _():
-                copy(s, tile).start()
-
-    @pl.when(slot == 0)
-    def _():
-        for s in range(min(buffers - 1, slots)):
-            start(s)
-
-    @pl.when(slot + buffers - 1 < slots)
-    def _():
-        start(slot + buffers - 1)
-
-    limit = limit_ref[slot]
-    place = lax.rem(slot, buffers)
-    data = data_ref[0]
-    half = data.shape[0] // 2
-    shape = out_ref.shape[1:3] + (KTILE,)
+                fetch(slot, n).start()
+
+    ahead = min(buffers - 1, end - begin)
+    for i in range(ahead):
+        start(begin + i)
     degree = lax.broadcasted_iota(jnp.int32, (half, KTILE), 1)
     parity = (1 - 2 * (degree % 2)).astype(jnp.float32)
-    for tile in range(tiles):
-        cols = pl.ds(tile * KTILE, KTILE)
-
-        @pl.when(tile * KTILE < limit)
+
+    def one(slot, carry):
+        @pl.when(slot + ahead < end)
         def _():
-            copy(slot, tile).wait()
-            product = lax.dot_general(
-                data, held[place, cols, :], (((1,), (1,)), ((), ())), preferred_element_type=jnp.float32
-            )
-            both = product[:half] + parity * product[half:]
-            both = jnp.where(degree < limit - tile * KTILE, both, 0.0)
-            out_ref[0, :, :, cols] = both.reshape(shape)
-
-        @pl.when(tile * KTILE >= limit)
+            start(slot + ahead)
+
+        limit = limit_ref[slot]
+        place, stage = lax.rem(slot, buffers), lax.rem(slot, stages)
+        count = tile_count(slot)
+        pieces = [ref[slot - base, h] for h in range(2) for ref, base in zip(data_refs, bases)]
+        data = jnp.concatenate(pieces, axis=0)
+
+        @pl.when(slot - begin >= stages)
         def _():
-            out_ref[0, :, :, cols] = jnp.zeros(shape, jnp.float32)
-
-
-def legendre_sum(limits, data, table, levels):
+            put(slot - stages).wait()
+
+        for n in range(1, tiles + 1):
+
+            @pl.when(count == n)
+            def _():
+                fetch(slot, n).wait()
+                product = lax.dot_general(
+                    data,
+                    held[place, 0 : n * KTILE, :],
+                    (((1,), (1,)), ((), ())),
+                    preferred_element_type=jnp.float32,
+                )
+                for t in range(n):
+                    cols = slice(t * KTILE, (t + 1) * KTILE)
+                    both = product[:half, cols] + parity * product[half:, cols]
+                    if t == n - 1:
+                        both = jnp.where(degree < limit - t * KTILE, both, 0.0)
+                    for chunk in range(len(bases)):
+                        for c in range(2):
+                            at = (chunk * 2 + c) * part
+                            staged[stage, c, chunk * part : (chunk + 1) * part, cols] = both[at : at + part]
+                if n < tiles:
+                    rest = (tiles - n) * KTILE
+                    staged[stage, :, :, n * KTILE :] = jnp.zeros((2, levels, rest), jnp.float32)
+
+        put(slot).start()
+        return carry
+
+    lax.fori_loop(begin, end, one, 0)
+    for slot in range(max(begin, end - stages), end):
+        put(slot).wait()
+
+
+def legendre_sum(limits, data, bases, table, begin, end, before):
     slots, degrees, lats = table.shape
-    columns = data.shape[1]
+    levels = sum(d.shape[2] for d in data) // 2
     tiles = degrees // KTILE
-    buffers = 6
+    anywhere = pl.BlockSpec(memory_space=pl.ANY)
+    vmem = pl.BlockSpec(memory_space=pltpu.VMEM)
+    operands = [limits, *data, table] + ([] if before is None else [before])
+    stages = min(4, end - begin)
     return pl.pallas_call(
-        functools.partial(legendre_kernel, slots, tiles, buffers),
-        grid_spec=pltpu.PrefetchScalarGridSpec(
-            num_scalar_prefetch=1,
-            grid=(slots,),
-            in_specs=[
-                pl.BlockSpec((1, columns, lats), lambda s, lim: (s, 0, 0)),
-                pl.BlockSpec(memory_space=pl.ANY),
-            ],
-            out_specs=pl.BlockSpec((1, 2, levels, degrees), lambda s, lim: (s, 0, 0, 0)),
-            scratch_shapes=[
-                pltpu.VMEM((buffers, degrees, lats), jnp.bfloat16),
-                pltpu.SemaphoreType.DMA((buffers, tiles)),
-            ],
-        ),
+        functools.partial(legendre_kernel, begin, end, tiles, bases, before is None),
         out_shape=jax.ShapeDtypeStruct((slots, 2, levels, degrees), jnp.float32),
+        in_specs=[pl.BlockSpec(memory_space=pltpu.SMEM)]
+        + [vmem] * len(data)
+        + [anywhere] * (1 if before is None else 2),
+        out_specs=anywhere,
+        scratch_shapes=[
+            pltpu.VMEM((6, degrees, lats), jnp.bfloat16),
+            pltpu.VMEM((stages, 2, levels, degrees), jnp.float32),
+            pltpu.SemaphoreType.DMA((6,)),
+            pltpu.SemaphoreType.DMA((stages,)),
+        ],
+        input_output_aliases={} if before is None else {len(operands) - 1: 0},
         compiler_params=pltpu.CompilerParams(vmem_limit_bytes=VMEM),
         cost_estimate=pl.CostEstimate(
-            flops=slots * degrees * lats * columns, bytes_accessed=slots * degrees * (lats + 64 * 2), transcendentals=0
+            flops=(end - begin) * degrees * lats * 4 * levels,
+            bytes_accessed=(end - begin) * degrees * (lats + 8 * levels),
+            transcendentals=0,
         ),
         name="legendre_sum",
-    )(limits, data, table)
+    )(*operands)
+
+
+def after(value, earlier):
+    return value if earlier is None else lax.optimization_barrier((value, earlier))[0]
+
+
+def spread(vorticity, chunk, lon_size, hop_order, earlier):
+    hemis, lats, part = vorticity.shape[1:]
+    me = lax.axis_index("lon")
+
+    def piece(distance):
+        level = chunk * lon_size + (me ^ distance)
+        block = lax.dynamic_index_in_dim(vorticity, level, 0, keepdims=False) * PRESCALE
+        return block.astype(jnp.float16).reshape(hemis * lats, part)
+
+    got = {0: piece(0)}
+    for distance in hop_order:
+        sent = after(piece(distance), earlier and earlier[distance])
+        got[distance] = lax.ppermute(sent, "lon", [(i, i ^ distance) for i in range(lon_size)])
+    return got
+
+
+def spread_whole(vorticity, chunk, lon_size, earlier):
+    hemis, lats, part = vorticity.shape[1:]
+    block = vorticity[chunk * lon_size : (chunk + 1) * lon_size] * PRESCALE
+    block = after(block.astype(jnp.float16).reshape(lon_size, hemis * lats, part), earlier)
+    return lax.all_to_all(block, "lon", split_axis=0, concat_axis=0, tiled=True)
 
 
 def on_device(lat_size, lon_size, high, low, vorticity, legendre, wave_order):
     levels, hemis, lats, part = vorticity.shape
     slot_count = legendre.shape[0]
+    devices = lat_size * lon_size
     waves = wave_order.astype(jnp.int32)
     lower, upper = waves % FIRST, waves // FIRST
     near = lower < HALF
     index = jnp.where(near, lower, FIRST - lower) * ROWS_K + jnp.where(near, 0, 2 * KEEP) + 2 * upper
     first_slot = lax.axis_index(("lat", "lon")) * slot_count
     limits = waves.shape[0] - lax.dynamic_slice_in_dim(waves, first_slot, slot_count)
+    me = lax.axis_index("lon").reshape(1)
     chunks = levels // lon_size
-    pieces = []
+    hop_order = sorted(range(1, lon_size), key=lambda d: (-(d >> 1), d & 1))
+
+    got = spread(vorticity, 0, lon_size, hop_order, None)
+    circles = [jnp.stack([got[i].astype(jnp.float32) for i in range(lon_size)])]
+    for chunk in range(1, chunks):
+        circles.append(spread_whole(vorticity, chunk, lon_size, tuple(got[d] for d in hop_order)).astype(jnp.float32))
+    done = None
+    arranged = []
     for chunk in range(chunks):
-        block = vorticity[chunk * lon_size : (chunk + 1) * lon_size] * PRESCALE
-        block = block.astype(jnp.float16).reshape(lon_size, hemis * lats, part)
-        block = lax.all_to_all(block, "lon", split_axis=0, concat_axis=0, tiled=True)
-        chosen = fourier_slots(block.astype(jnp.float32), index, high, low)
-        chosen = chosen.reshape(lat_size * lon_size, slot_count * 2, hemis * lats)
-        moved = lax.all_to_all(chosen, ("lat", "lon"), split_axis=0, concat_axis=0, tiled=True)
-        moved = moved.reshape(lat_size, lon_size, slot_count, 2, hemis, lats)
-        pieces.append(moved)
-    data = jnp.stack(pieces, axis=0)
-    data = jnp.transpose(data, (3, 5, 4, 0, 2, 1, 6)).reshape(slot_count, hemis * 2 * levels, lat_size * lats)
-    return legendre_sum(limits, data, legendre, levels)
+        parts = 2 if chunk == chunks - 1 else 1
+        order = index.reshape(devices, parts, slot_count // parts).transpose(1, 0, 2).reshape(-1)
+        pieces = []
+        origin = me if chunk == 0 else jnp.zeros_like(me)
+        results = fourier_slots(after(circles[chunk], done), origin, order, high, low, parts)
+        done = results[0]
+        for chosen in results:
+            chosen = chosen.reshape(devices, slot_count // parts * 2, hemis * lats)
+            moved = lax.all_to_all(chosen, ("lat", "lon"), split_axis=0, concat_axis=0, tiled=True)
+            pieces.append(arrange(moved, lat_size, lon_size, slot_count // parts))
+        arranged.append(pieces)
+    result = None
+    half = slot_count // 2
+    for part in range(2):
+        begin = part * half
+        data = [pieces[part] if len(pieces) == 2 else pieces[0] for pieces in arranged]
+        bases = [begin if len(pieces) == 2 else 0 for pieces in arranged]
+        result = legendre_sum(limits, data, bases, legendre, begin, begin + half, result)
+    return result
 
 
 def solution(mesh):

time: 277 us -> 199 us (0.72)
  blocking collectives: 55.5 us -> 19.7 us
  starting transfers between devices: 10.6 us -> 44.9 us
  Pallas kernels: 104 us -> 70.3 us
  local copies, waits for them, and re-layouts: 23.4 us -> 4.8 us
  waiting for transfers between devices: 57.5 us -> 44.6 us
  other arithmetic: 22.6 us -> 13.1 us
    all_to_all x1, blocking collectives: 55.5 us -> 19.7 us  [on_device(): lax.all_to_all(chosen, ('lat', 'lon'), split_axis=0, concat_axis=0, tiled...]
    ppermute x0 -> x7, starting transfers between devices: none -> 35 us  [spread(): lax.ppermute(sent, 'lon', [(i, i ^ distance) for i in range(lon_size)])]
    pallas_call x3 -> x7, Pallas kernels: 104 us -> 70.3 us  [the longest x2 33.8 us: fourier_slots(): pl.pallas_call(functools.partial(fourier_kernel, rows, slots, parts), out...]
    all_to_all x2, waiting for transfers between devices: 31.2 us -> 7.38 us  [on_device(): lax.all_to_all(chosen, ('lat', 'lon'), split_axis=0, concat_axis=0, tiled...]
    ppermute x0 -> x7, waiting for transfers between devices: none -> 12.9 us  [spread(): lax.ppermute(sent, 'lon', [(i, i ^ distance) for i in range(lon_size)])]
    another operation x2 -> x1, local copies, waits for them, and re-layouts: 8.84 us -> 0.05 us  [on_device(): circles = [jnp.stack([got[i].astype(jnp.float32) for i in range(lon_size)])]]
    transpose x1 -> x0, other arithmetic: 8.6 us -> none  [on_device(): jnp.transpose(data, (3, 5, 4, 0, 2, 1, 6))]
    transpose x1, local copies, waits for them, and re-layouts: 7.63 us -> 0.01 us  [on_device(): index.reshape(devices, parts, slot_count // parts).transpose(1, 0, 2)]
  transfers between devices with their start and end apart: 3 -> 10, of which waited for: 3 -> 5; matrix products, arithmetic and copies ran while one was open for 4% -> 7% of each run, Pallas kernels for 12% -> 27%
where the time goes in v2:
time: 199 us; the launch traced here: 198 us
  Pallas kernels  70.3 us (35%)
  starting transfers between devices  44.9 us (23%)
  waiting for transfers between devices  44.6 us (22%)
  blocking collectives  19.7 us (10%)
  other arithmetic  13.1 us (7%)
  local copies, waits for them, and re-layouts  4.8 us (2%)
    ppermute x7, starting transfers between devices, spread(): lax.ppermute(sent, 'lon', [(i, i ^ distance) for i in range(lon_size)])  35 us
    pallas_call x2, Pallas kernels, fourier_slots(): pl.pallas_call(functools.partial(fourier_kernel, rows, slots, parts), out...  33.8 us
    pallas_call x2, Pallas kernels, legendre_sum(): pl.pallas_call(functools.partial(legendre_kernel, begin, end, tiles, base...  29.4 us
    all_to_all x1, waiting for transfers between devices, spread_whole(): return lax.all_to_all(block, 'lon', split_axis=0, concat_axis=0, tiled=True)  24.4 us
    all_to_all x1, blocking collectives, on_device(): lax.all_to_all(chosen, ('lat', 'lon'), split_axis=0, concat_axis=0, tiled...  19.7 us
    ppermute x7, waiting for transfers between devices, spread(): lax.ppermute(sent, 'lon', [(i, i ^ distance) for i in range(lon_size)])  12.9 us
    all_to_all x2, waiting for transfers between devices, on_device(): lax.all_to_all(chosen, ('lat', 'lon'), split_axis=0, concat_axis=0, tiled...  7.38 us
    pallas_call x3, Pallas kernels, arrange(): pl.pallas_call(functools.partial(arrange_kernel, lat_size, lon_size, slot...  7.13 us
  transfers between devices with their start and end apart: 10, of which 5 were waited for; matrix products, arithmetic and copies ran while one was open for 7% of the time, Pallas kernels for 27%

profile of v2, /device:TPU:0, one launch (start us, length us, event | category | flops | bytes accessed | tf_op | source)
XLA Modules:
  0.0 197.6 jit_solution(5894294368607306989)
XLA Ops:
  0.0 2.7 %multiply_convert_fusion.1 = (f16[1,2,64,1024]{3,2,1,0:T(8,128)(2,1)S(1)}, f16[1,2,64,1024]{3,2,1,0:T(8,128)(2,1)S(1)}, f16[1,2,64,1024]{3,2,1,0:T(8,128)(2,1)S(...) fusion(f32[16,2,64,1024]{3,2,1,0:T(8,128)} %param.5, ...), kind=kLoop, calls=%fused_computation.1 | loop fusion | flops 2097152 | bytes 6291488 | tf_op jit(solution)/shard_map/convert_element_type | solution.py:354
  2.7 5.1 %collective-permute-start.5 = (f16[128,1024]{1,0:T(8,128)(2,1)S(1)}, f16[128,1024]{1,0:T(8,128)(2,1)S(1)}, u32[]{:S(2)}, u32[]{:S(2)}) collective-permute-start(f16[128,1024]{1,0:T(8,128)(2,1)S(1)} %bitcast.38), channel_id=1, source_target_pairs={{0,6},{1,7},{2,4},{3,5},{4,2},{5,3},{6,0},{7,1},{8,14},{9,15},{10,... | collective-permute-start | bytes 786440 | tf_op jit(solution)/shard_map/ppermute | solution.py:359
  7.8 1.2 collective-permute-start.6
  9.0 0.7 collective-permute-start.4
  9.8 2.0 %collective-permute-start.3 = (f16[128,1024]{1,0:T(8,128)(2,1)S(1)}, f16[128,1024]{1,0:T(8,128)(2,1)S(1)}, u32[]{:S(2)}, u32[]{:S(2)}) collective-permute-start(f16[128,1024]{1,0:T(8,128)(2,1)S(1)} %bitcast.35), channel_id=1, source_target_pairs={{0,4},{1,5},{2,6},{3,7},{4,0},{5,1},{6,2},{7,3},{8,12},{9,13},{10,... | collective-permute-start | bytes 786440 | tf_op jit(solution)/shard_map/ppermute | solution.py:359
  11.7 2.3 %collective-permute-start.2 = (f16[128,1024]{1,0:T(8,128)(2,1)S(1)}, f16[128,1024]{1,0:T(8,128)(2,1)}, u32[]{:S(2)}, u32[]{:S(2)}) collective-permute-start(f16[128,1024]{1,0:T(8,128)(2,1)S(1)} %bitcast.34), channel_id=1, source_target_pairs={{0,3},{1,2},{2,1},{3,0},{4,7},{5,6},{6,5},{7,4},{8,11},{9,10},{10,... | collective-permute-start | bytes 786440 | tf_op jit(solution)/shard_map/ppermute | solution.py:359
  14.1 1.1 collective-permute-done.5
  15.2 22.1 %collective-permute-start.1 = (f16[128,1024]{1,0:T(8,128)(2,1)S(1)}, f16[128,1024]{1,0:T(8,128)(2,1)}, u32[]{:S(2)}, u32[]{:S(2)}) collective-permute-start(f16[128,1024]{1,0:T(8,128)(2,1)S(1)} %bitcast.33), channel_id=1, source_target_pairs={{0,2},{1,3},{2,0},{3,1},{4,6},{5,7},{6,4},{7,5},{8,10},{9,11},{10,... | collective-permute-start | bytes 786440 | tf_op jit(solution)/shard_map/ppermute | solution.py:359
  37.3 0.0 collective-permute-done.6
  37.3 1.5 collective-permute-start
  38.8 4.1 %multiply_convert_fusion = f16[8,2,64,1024]{3,2,1,0:T(8,128)(2,1)} fusion(f32[16,2,64,1024]{3,2,1,0:T(8,128)} %param.5), kind=kLoop, calls=%fused_computation | loop fusion | flops 2097152 | bytes 6291456 | tf_op jit(solution)/shard_map/convert_element_type | solution.py:366
  42.9 8.0 %collective-permute-done.4 = f16[128,1024]{1,0:T(8,128)(2,1)S(1)} collective-permute-done((f16[128,1024]{1,0:T(8,128)(2,1)S(1)}, f16[128,1024]{1,0:T(8,128)(2,1)S(1)}, u32[]{:S(2)}, u32[]{:S(2)}) %collective-permute-start.4) | collective-permute-done | bytes 262176 | tf_op jit(solution)/shard_map/ppermute | solution.py:359
  51.0 3.7 %collective-permute-done.3 = f16[128,1024]{1,0:T(8,128)(2,1)S(1)} collective-permute-done((f16[128,1024]{1,0:T(8,128)(2,1)S(1)}, f16[128,1024]{1,0:T(8,128)(2,1)S(1)}, u32[]{:S(2)}, u32[]{:S(2)}) %collective-permute-start.3) | collective-permute-done | bytes 262176 | tf_op jit(solution)/shard_map/ppermute | solution.py:359
  54.7 0.0 collective-permute-done.2
  54.7 0.0 collective-permute-done.1
  54.7 0.0 collective-permute-done
  54.7 0.0 copy-start.3
  54.8 3.6 %all-to-all-start.1 = ((f16[8,128,1024]{2,1,0:T(8,128)(2,1)}), f16[8,128,1024]{2,1,0:T(8,128)(2,1)S(1)}, u32[]{:S(2)}, u32[]{:S(2)}) async-start(f16[8,128,1024]{2,1,0:T(8,128)(2,1)} %bitcast.18), calls=%async_computation.1 | async-start | bytes 4194304 | tf_op jit(solution)/shard_map/all_to_all | solution.py:367
  58.4 0.0 copy-done.3
  58.4 0.6 fusion.1.index_ref
  59.0 1.0 bitcast_dynamic-update-slice_fusion.6
  60.0 1.0 bitcast_dynamic-update-slice_fusion.5
  61.1 1.0 bitcast_dynamic-update-slice_fusion.4
  62.3 2.5 %stack.42.x_ref = f32[8,128,1024]{2,1,0:T(8,128)} convert(f16[8,128,1024]{2,1,0:T(8,128)(2,1)S(1)} %bitcast_dynamic-update-slice_fusion) | non-fusion elementwise | flops 1048576 | bytes 6291456 | tf_op jit(solution)/shard_map/stack | solution.py:385
  64.8 16.9 %fourier_slots.2 = bf16[4096,128]{1,0:T(8,128)(2,1)} custom-call(s32[2048]{0:T(1024)} %fusion.1.index_ref, s32[1]{0:T(128)} %bitcast.me_ref, f32[8,128,1024]{2,1,0:T(8,128)} %stack.42.x_ref, bf16[33,128,256]{2,1,0:T(8,128)(2,1)} %constant.88.clone.high_ref, bf16[33,128,256]{2,1,0:T(8,128)(2,1)} %constant.89.clone.low_ref), custom_call_target="tpu_custom_call" | custom-call | flops 830472192 | bytes 12582912 | tf_op jit(solution)/shard_map/fourier_slots/pallas_call | solution.py:171
  81.7 0.0 copy-start.2
  81.7 24.4 %all-to-all-done.1 = f16[8,128,1024]{2,1,0:T(8,128)(2,1)S(1)} async-done(((f16[8,128,1024]{2,1,0:T(8,128)(2,1)}), f16[8,128,1024]{2,1,0:T(8,128)(2,1)S(1)}, u32[]{:S(2)}, u32[]{:S(2)}) %all-to-all-start.1) | async-done | bytes 2097184 | tf_op jit(solution)/shard_map/all_to_all | solution.py:367
  106.1 3.6 %all-to-all-start = ((bf16[32,128,128]{2,1,0:T(8,128)(2,1)}), bf16[32,128,128]{2,1,0:T(8,128)(2,1)S(1)}, u32[]{:S(2)}, u32[]{:S(2)}) async-start(bf16[32,128,128]{2,1,0:T(8,128)(2,1)} %bitcast.28), calls=%async_computation | async-start | bytes 2097152 | tf_op jit(solution)/shard_map/all_to_all | solution.py:399
  109.7 0.0 copy-done.2
  109.7 0.1 reshape.81
  109.8 0.7 reshape.82.index_ref
  110.5 2.5 %convert_element_type.102.x_ref = f32[8,128,1024]{2,1,0:T(8,128)} convert(f16[8,128,1024]{2,1,0:T(8,128)(2,1)S(1)} %all-to-all-done.1) | non-fusion elementwise | flops 1048576 | bytes 6291456 | tf_op jit(solution)/shard_map/convert_element_type | solution.py:387
  113.0 16.9 %fourier_slots.3 = (bf16[2048,128]{1,0:T(8,128)(2,1)}, bf16[2048,128]{1,0:T(8,128)(2,1)}) custom-call(s32[2048]{0:T(1024)} %reshape.82.index_ref, s32[1]{0:T(128)} %constant.87.clone.1.me_ref, f32[8,128,1024]{2,1,0:T(8,128)} %convert_element_type.102.x_ref, bf16[33,128,256]{2,1,0:T(8,128)(2,1)} %constant.88.clone.high_ref, ...), custom_call_target="tpu_custom_call" | custom-call | flops 830472192 | bytes 12582912 | tf_op jit(solution)/shard_map/fourier_slots/pallas_call | solution.py:171
  129.9 7.4 %all-to-all-done.moved_ref = bf16[32,128,128]{2,1,0:T(8,128)(2,1)S(1)} async-done(((bf16[32,128,128]{2,1,0:T(8,128)(2,1)}), bf16[32,128,128]{2,1,0:T(8,128)(2,1)S(1)}, u32[]{:S(2)}, u32[]{:S(2)}) %all-to-all-start) | async-done | bytes 1048608 | tf_op jit(solution)/shard_map/all_to_all | solution.py:399
  137.3 0.0 copy-start
  137.3 19.7 %all_to_all.20.moved_ref = bf16[32,64,128]{2,1,0:T(8,128)(2,1)} all-to-all(bf16[32,64,128]{2,1,0:T(8,128)(2,1)} %bitcast.31), channel_id=1, replica_groups=mesh['lat'=4,'lon'=8] {'lat','lon'}, dimensions={0} | all-to-all | bytes 1048576 | tf_op jit(solution)/shard_map/all_to_all | solution.py:399
  157.0 2.6 %all-to-all-start.2 = ((bf16[32,64,128]{2,1,0:T(8,128)(2,1)}), bf16[32,64,128]{2,1,0:T(8,128)(2,1)S(1)}, u32[]{:S(2)}, u32[]{:S(2)}) async-start(bf16[32,64,128]{2,1,0:T(8,128)(2,1)} %bitcast.30), calls=%async_computation.2 | async-start | bytes 1048576 | tf_op jit(solution)/shard_map/all_to_all | solution.py:399
  159.6 0.6 dynamic-slice_subtract_fusion.refs_0_
  160.2 0.0 copy-done
  160.2 2.8 %arrange.3.refs_1_ = bf16[64,2,16,256]{3,2,1,0:T(8,128)(2,1)} custom-call(bf16[32,128,128]{2,1,0:T(8,128)(2,1)} %copy-done), custom_call_target="tpu_custom_call" | custom-call | flops 1024 | bytes 16777216 | tf_op jit(solution)/shard_map/arrange/pallas_call | solution.py:216
  163.0 2.2 %arrange.5.refs_2_ = bf16[32,2,16,256]{3,2,1,0:T(8,128)(2,1)} custom-call(bf16[32,64,128]{2,1,0:T(8,128)(2,1)} %all_to_all.20.moved_ref), custom_call_target="tpu_custom_call" | custom-call | flops 1024 | bytes 16777216 | tf_op jit(solution)/shard_map/arrange/pallas_call | solution.py:216
  165.2 14.6 %legendre_sum.2.refs_4_ = f32[64,2,16,2048]{3,2,1,0:T(8,128)} custom-call(s32[64]{0:T(128)} %dynamic-slice_subtract_fusion.refs_0_, bf16[64,2,16,256]{3,2,1,0:T(8,128)(2,1)} %arrange.3.refs_1_, bf16[32,2,16,256]{3,2,1,0:T(8,128)(2,1)} %arrange.5.refs_2_, bf16[64,2048,256]{2,1,0:T(8,128)(2,1)} %refs_3_.3), custom_call_target="tpu_custom_call" | custom-call | flops 1073741824 | bytes 25165824 | tf_op jit(solution)/shard_map/legendre_sum/pallas_call | solution.py:319
  179.8 0.0 all-to-all-done.2.moved_ref
  179.8 0.0 copy-start.1
  179.8 0.8 copy-done.1
  180.6 2.2 %arrange.4.refs_2_ = bf16[32,2,16,256]{3,2,1,0:T(8,128)(2,1)} custom-call(bf16[32,64,128]{2,1,0:T(8,128)(2,1)} %copy-done.1), custom_call_target="tpu_custom_call" | custom-call | flops 1024 | bytes 16777216 | tf_op jit(solution)/shard_map/arrange/pallas_call | solution.py:216
  182.8 14.8 %legendre_sum.3 = f32[64,2,16,2048]{3,2,1,0:T(8,128)} custom-call(s32[64]{0:T(128)} %dynamic-slice_subtract_fusion.refs_0_, bf16[64,2,16,256]{3,2,1,0:T(8,128)(2,1)} %arrange.3.refs_1_, bf16[32,2,16,256]{3,2,1,0:T(8,128)(2,1)} %arrange.4.refs_2_, bf16[64,2048,256]{2,1,0:T(8,128)(2,1)} %refs_3_.3, ...), custom_call_target="tpu_custom_call", output_to_operand_aliasing={{}: (4, {})} | custom-call | flops 1073741824 | bytes 25165824 | tf_op jit(solution)/shard_map/legendre_sum/pallas_call | solution.py:319
  (6 shorter events, 0.2 us)
Async XLA Ops:
  2.7 12.4 %collective-permute-start.5 = (f16[128,1024]{1,0:T(8,128)(2,1)S(1)}, f16[128,1024]{1,0:T(8,128)(2,1)S(1)}, u32[]{:S(2)}, u32[]{:S(2)}) collective-permute-start(f16[128,1024]{1,0:T(8,128)(2,1)S(1)} %bitcast.38), channel_id=1, source_target_pairs={{0,6},{1,7},{2,4},{3,5},{4,2},{5,3},{6,0},{7,1},{8,14},{9,15},{10,... | collective-permute-start | bytes 786440 | tf_op jit(solution)/shard_map/ppermute | solution.py:359
  7.8 29.5 %collective-permute-start.6 = (f16[128,1024]{1,0:T(8,128)(2,1)S(1)}, f16[128,1024]{1,0:T(8,128)(2,1)S(1)}, u32[]{:S(2)}, u32[]{:S(2)}) collective-permute-start(f16[128,1024]{1,0:T(8,128)(2,1)S(1)} %bitcast.37), channel_id=1, source_target_pairs={{0,7},{1,6},{2,5},{3,4},{4,3},{5,2},{6,1},{7,0},{8,15},{9,14},{10,... | collective-permute-start | bytes 786440 | tf_op jit(solution)/shard_map/ppermute | solution.py:359
  9.0 42.0 %collective-permute-start.4 = (f16[128,1024]{1,0:T(8,128)(2,1)S(1)}, f16[128,1024]{1,0:T(8,128)(2,1)S(1)}, u32[]{:S(2)}, u32[]{:S(2)}) collective-permute-start(f16[128,1024]{1,0:T(8,128)(2,1)S(1)} %bitcast.36), channel_id=1, source_target_pairs={{0,5},{1,4},{2,7},{3,6},{4,1},{5,0},{6,3},{7,2},{8,13},{9,12},{10,... | collective-permute-start | bytes 786440 | tf_op jit(solution)/shard_map/ppermute | solution.py:359
  9.8 45.0 %collective-permute-start.3 = (f16[128,1024]{1,0:T(8,128)(2,1)S(1)}, f16[128,1024]{1,0:T(8,128)(2,1)S(1)}, u32[]{:S(2)}, u32[]{:S(2)}) collective-permute-start(f16[128,1024]{1,0:T(8,128)(2,1)S(1)} %bitcast.35), channel_id=1, source_target_pairs={{0,4},{1,5},{2,6},{3,7},{4,0},{5,1},{6,2},{7,3},{8,12},{9,13},{10,... | collective-permute-start | bytes 786440 | tf_op jit(solution)/shard_map/ppermute | solution.py:359
  11.7 43.0 %collective-permute-start.2 = (f16[128,1024]{1,0:T(8,128)(2,1)S(1)}, f16[128,1024]{1,0:T(8,128)(2,1)}, u32[]{:S(2)}, u32[]{:S(2)}) collective-permute-start(f16[128,1024]{1,0:T(8,128)(2,1)S(1)} %bitcast.34), channel_id=1, source_target_pairs={{0,3},{1,2},{2,1},{3,0},{4,7},{5,6},{6,5},{7,4},{8,11},{9,10},{10,... | collective-permute-start | bytes 786440 | tf_op jit(solution)/shard_map/ppermute | solution.py:359
  15.2 39.6 %collective-permute-start.1 = (f16[128,1024]{1,0:T(8,128)(2,1)S(1)}, f16[128,1024]{1,0:T(8,128)(2,1)}, u32[]{:S(2)}, u32[]{:S(2)}) collective-permute-start(f16[128,1024]{1,0:T(8,128)(2,1)S(1)} %bitcast.33), channel_id=1, source_target_pairs={{0,2},{1,3},{2,0},{3,1},{4,6},{5,7},{6,4},{7,5},{8,10},{9,11},{10,... | collective-permute-start | bytes 786440 | tf_op jit(solution)/shard_map/ppermute | solution.py:359
  37.3 17.4 %collective-permute-start = (f16[128,1024]{1,0:T(8,128)(2,1)S(1)}, f16[128,1024]{1,0:T(8,128)(2,1)}, u32[]{:S(2)}, u32[]{:S(2)}) collective-permute-start(f16[128,1024]{1,0:T(8,128)(2,1)S(1)} %bitcast.32), channel_id=1, source_target_pairs={{0,1},{1,0},{2,3},{3,2},{4,5},{5,4},{6,7},{7,6},{8,9},{9,8},{10,11... | collective-permute-start | bytes 786440 | tf_op jit(solution)/shard_map/ppermute | solution.py:359
  54.7 3.7 %copy-start.3 = (s32[2048]{0:T(1024)S(1)}, s32[2048]{0:T(1024)}, u32[]{:S(2)}) copy-start(s32[2048]{0:T(1024)} %param.7) | copy-start | bytes 24580
  54.8 51.3 %all-to-all-start.1 = ((f16[8,128,1024]{2,1,0:T(8,128)(2,1)}), f16[8,128,1024]{2,1,0:T(8,128)(2,1)S(1)}, u32[]{:S(2)}, u32[]{:S(2)}) async-start(f16[8,128,1024]{2,1,0:T(8,128)(2,1)} %bitcast.18), calls=%async_computation.1 | async-start | bytes 4194304 | tf_op jit(solution)/shard_map/all_to_all | solution.py:367
  81.7 28.0 %copy-start.2 = (s32[2048]{0:T(1024)S(1)}, s32[2048]{0:T(1024)}, u32[]{:S(2)}) copy-start(s32[2048]{0:T(1024)} %fusion.1.index_ref) | copy-start | bytes 24580
  106.1 31.2 %all-to-all-start = ((bf16[32,128,128]{2,1,0:T(8,128)(2,1)}), bf16[32,128,128]{2,1,0:T(8,128)(2,1)S(1)}, u32[]{:S(2)}, u32[]{:S(2)}) async-start(bf16[32,128,128]{2,1,0:T(8,128)(2,1)} %bitcast.28), calls=%async_computation | async-start | bytes 2097152 | tf_op jit(solution)/shard_map/all_to_all | solution.py:399
  137.3 22.9 %copy-start = (bf16[32,128,128]{2,1,0:T(8,128)(2,1)}, bf16[32,128,128]{2,1,0:T(8,128)(2,1)S(1)}, u32[]{:S(2)}) copy-start(bf16[32,128,128]{2,1,0:T(8,128)(2,1)S(1)} %all-to-all-done.moved_ref) | copy-start | bytes 3145732
  157.0 22.8 %all-to-all-start.2 = ((bf16[32,64,128]{2,1,0:T(8,128)(2,1)}), bf16[32,64,128]{2,1,0:T(8,128)(2,1)S(1)}, u32[]{:S(2)}, u32[]{:S(2)}) async-start(bf16[32,64,128]{2,1,0:T(8,128)(2,1)} %bitcast.30), calls=%async_computation.2 | async-start | bytes 1048576 | tf_op jit(solution)/shard_map/all_to_all | solution.py:399
  179.8 0.8 copy-start.1

commit v3 on v2

v3 whole, which is shorter than its diff:
```python
import functools
import math

import jax
import jax.numpy as jnp
import numpy as np
from jax import lax
from jax.experimental import pallas as pl
from jax.experimental.pallas import tpu as pltpu
from jax.sharding import PartitionSpec as P

MW = 2048
FIRST = 64
LANES = 128
KEEP = MW // FIRST
HALF = FIRST // 2 + 1
ROWS_K = 4 * KEEP
KTILE = 256
PRESCALE = 8192.0
VMEM = 56 * 1024 * 1024
GROUP = 32
BUFFERS = 32


def second_tables(circle):
    b = np.arange(LANES)[None, :]
    scale = 1.0 / math.sqrt(circle) / PRESCALE
    table = np.zeros((HALF, 2, KEEP, 2, 2 * LANES), np.float64)
    for k in range(HALF):
        for side in range(2):
            first = k if side == 0 else FIRST - k
            m = (first + FIRST * np.arange(KEEP))[:, None]
            angle = 2.0 * np.pi / circle * ((m * b) % circle)
            c, s = np.cos(angle), np.sin(angle)
            sign = 1.0 if side == 0 else -1.0
            table[k, side, :, 0, :LANES] = c
            table[k, side, :, 0, LANES:] = sign * s
            table[k, side, :, 1, :LANES] = -s
            table[k, side, :, 1, LANES:] = sign * c
    table = (table * scale).astype(np.float32).reshape(HALF, ROWS_K, 2 * LANES)
    high = table.astype(jnp.bfloat16)
    low = (table - high.astype(np.float32)).astype(jnp.bfloat16)
    return high, low


def add(a, b):
    return (a[0] + b[0], a[1] + b[1])


def sub(a, b):
    return (a[0] - b[0], a[1] - b[1])


def minus_i(a):
    return (a[1], -a[0])


def times(a, angle):
    c, s = math.cos(angle), math.sin(angle)
    return (a[0] * c + a[1] * s, a[1] * c - a[0] * s)


def real_dft8(x):
    r = math.sqrt(0.5)
    s04, d04 = x[0] + x[4], x[0] - x[4]
    s26, d26 = x[2] + x[6], x[2] - x[6]
    s15, d15 = x[1] + x[5], x[1] - x[5]
    s37, d37 = x[3] + x[7], x[3] - x[7]
    even, odd = s04 + s26, s15 + s37
    p, q = r * (d15 - d37), r * (d15 + d37)
    return [
        (even + odd, None),
        (d04 + p, -(d26 + q)),
        (s04 - s26, -(s15 - s37)),
        (d04 - p, d26 - q),
        (even - odd, None),
    ]


def complex_dft8(x):
    r = math.sqrt(0.5)

    def dft4(a, b, c, d):
        s, t, u, v = add(a, c), sub(a, c), add(b, d), minus_i(sub(b, d))
        return [add(s, u), add(t, v), sub(s, u), sub(t, v)]

    even = dft4(x[0], x[2], x[4], x[6])
    odd = dft4(x[1], x[3], x[5], x[7])
    o1 = ((odd[1][0] + odd[1][1]) * r, (odd[1][1] - odd[1][0]) * r)
    o2 = minus_i(odd[2])
    o3 = ((odd[3][1] - odd[3][0]) * r, -(odd[3][0] + odd[3][1]) * r)
    turned = [odd[0], o1, o2, o3]
    return [add(e, o) for e, o in zip(even, turned)] + [sub(e, o) for e, o in zip(even, turned)]


def fourier_kernel(
    rows, slots, index_ref, me_ref, x_ref, high_ref, low_ref, out_ref, stage, y_high, y_low, full, picked
):
    me = me_ref[0]
    per_source = x_ref.shape[2] // LANES
    group = 16

    def put(k, row, value):
        for part in range(2):
            at = (k, pl.ds(row, group), pl.ds(part * LANES, LANES))
            v = value[part]
            if v is None:
                v = jnp.zeros((group, LANES), jnp.float32)
            h = v.astype(jnp.bfloat16)
            y_high[at] = h
            y_low[at] = (v - h.astype(jnp.float32)).astype(jnp.bfloat16)

    def first_step(step, carry):
        row = pl.multiple_of(step * group, group)
        for t in range(8):
            x = []
            for s in range(8):
                source, piece = divmod(8 * s + t, per_source)
                x.append(x_ref[me ^ source, pl.ds(row, group), pl.ds(piece * LANES, LANES)])
            for k1, (real, imag) in enumerate(real_dft8(x)):
                stage[t, k1, 0] = real
                if imag is not None:
                    stage[t, k1, 1] = imag
        for k2, value in enumerate(real_dft8([stage[t, 0, 0] for t in range(8)])):
            put(8 * k2, row, value)
        for k1 in range(1, 5):
            turned = []
            for t in range(8):
                angle = 2.0 * math.pi * t * k1 / FIRST
                if k1 == 4:
                    real = stage[t, k1, 0]
                    turned.append((real * math.cos(angle), real * -math.sin(angle)))
                else:
                    turned.append(times((stage[t, k1, 0], stage[t, k1, 1]), angle))
            for k2, value in enumerate(complex_dft8(turned)):
                k = k1 + 8 * k2
                if k < HALF:
                    put(k, row, value)
                elif k1 != 4:
                    put(FIRST - k, row, (value[0], -value[1]))
        return carry

    lax.fori_loop(0, rows // group, first_step, 0)

    def dot(a, b):
        return lax.dot_general(a, b, (((1,), (1,)), ((), ())), preferred_element_type=jnp.float32)

    def second_step(k, carry):
        at = pl.ds(pl.multiple_of(k * ROWS_K, ROWS_K), ROWS_K)
        full[at, :] = dot(high_ref[k], y_high[k]) + (dot(high_ref[k], y_low[k]) + dot(low_ref[k], y_high[k]))
        return carry

    lax.fori_loop(0, HALF, second_step, 0)

    def pick(step, carry):
        first = step * 8
        for i in range(8):
            at = pl.multiple_of(index_ref[first + i], 2)
            to = pl.multiple_of(step * 16, 16) + 2 * i
            picked[pl.ds(to, 2), :] = full[pl.ds(at, 2), :]
        return carry

    lax.fori_loop(0, slots // 8, pick, 0)
    out_ref[...] = picked[...].astype(jnp.bfloat16)


def fourier_slots(x, me, index, high, low):
    sources, rows, part = x.shape
    slots = index.shape[0]
    smem, vmem = pl.BlockSpec(memory_space=pltpu.SMEM), pl.BlockSpec(memory_space=pltpu.VMEM)
    return pl.pallas_call(
        functools.partial(fourier_kernel, rows, slots),
        out_shape=jax.ShapeDtypeStruct((slots * 2, rows), jnp.bfloat16),
        in_specs=[smem, smem, vmem, vmem, vmem],
        out_specs=vmem,
        scratch_shapes=[
            pltpu.VMEM((8, 5, 2, 16, LANES), jnp.float32),
            pltpu.VMEM((HALF, rows, 2 * LANES), jnp.bfloat16),
            pltpu.VMEM((HALF, rows, 2 * LANES), jnp.bfloat16),
            pltpu.VMEM((HALF * ROWS_K, rows), jnp.float32),
            pltpu.VMEM((slots * 2, rows), jnp.float32),
        ],
        compiler_params=pltpu.CompilerParams(vmem_limit_bytes=VMEM),
        cost_estimate=pl.CostEstimate(
            flops=6 * HALF * ROWS_K * rows * 2 * LANES, bytes_accessed=12 * 1024 * 1024, transcendentals=0
        ),
        name="fourier_slots",
    )(index, me, x, high, low)


def arrange(moved, slots, lat_size, lon_size):
    lats = moved.shape[2] // 2
    moved = moved.reshape(lat_size, lon_size, slots, 2, 2, lats)
    moved = jnp.transpose(moved, (2, 4, 3, 1, 0, 5))
    return moved.reshape(slots, 4 * lon_size, lat_size * lats)


def arrange_here(lat_size, lon_size, moved_ref, data_ref, sorted_rows):
    slots = data_ref.shape[0]
    rows = slots * 2
    for lat in range(lat_size):
        for lon in range(lon_size):
            block = moved_ref[lat * lon_size + lon].astype(jnp.float32)
            sorted_rows[lat, pl.ds(lon, rows, stride=lon_size), :] = block
    shape = (slots, 2 * lon_size, LANES)
    lane = lax.broadcasted_iota(jnp.int32, (rows * lon_size, LANES), 1)
    lower = lane < LANES // 2
    for pair in range(lat_size // 2):
        one, two = sorted_rows[2 * pair], sorted_rows[2 * pair + 1]
        north = jnp.where(lower, one, pltpu.roll(two, LANES // 2, 1))
        south = jnp.where(lower, pltpu.roll(one, LANES // 2, 1), two)
        lanes = pl.ds(pair * LANES, LANES)
        data_ref[:, 0 : 2 * lon_size, lanes] = north.reshape(shape).astype(jnp.bfloat16)
        data_ref[:, 2 * lon_size : 4 * lon_size, lanes] = south.reshape(shape).astype(jnp.bfloat16)


def legendre_kernel(tiles, level, sizes, has_before, limit_ref, moved_ref, table_ref, *refs):
    out_ref, held, staged, slot_of, tile_of, last_of, in_sems, out_sems, *scratch = refs[1 if has_before else 0 :]
    data_ref = scratch[0]
    incoming = pltpu.make_async_copy(moved_ref, scratch[2] if sizes else data_ref, scratch[-1])
    incoming.start()
    buffers, stages = held.shape[0], staged.shape[0]
    levels = staged.shape[2]
    half = 2 * levels
    begin, end = 0, table_ref.shape[0]

    def tile_count(slot):
        return lax.div(limit_ref[slot] + (KTILE - 1), KTILE)

    def fetch(slot, count):
        place = lax.rem(slot, buffers)
        rows = pl.ds(0, count * KTILE)
        return pltpu.make_async_copy(table_ref.at[slot, rows, :], held.at[place, rows, :], in_sems.at[place])

    def put(slot):
        place = lax.rem(slot, stages)
        target = out_ref.at[slot, :, pl.ds(level, levels), :]
        return pltpu.make_async_copy(staged.at[place], target, out_sems.at[place])

    def by_count(slot, act):
        count = tile_count(slot)

        def choose(low, high):
            if low == high:
                act(fetch(slot, low))
                return
            middle = (low + high) // 2
            lax.cond(count <= middle, lambda: choose(low, middle), lambda: choose(middle + 1, high))

        choose(1, tiles)

    def start(slot, carry):
        by_count(slot, lambda copy: copy.start())
        return carry

    lax.fori_loop(begin, min(begin + buffers, end), start, 0)

    def list_slot(slot, total):
        def list_tile(tile, carry):
            slot_of[total + tile] = slot
            tile_of[total + tile] = tile
            return carry

        count = tile_count(slot)
        lax.fori_loop(0, count, list_tile, 0)
        last_of[slot - begin] = total + count
        return total + count

    total = lax.fori_loop(begin, end, list_slot, 0)
    final = tile_of[total - 1]
    for i in range(GROUP):
        slot_of[total + i] = end - 1
        tile_of[total + i] = final

    incoming.wait()
    if sizes:
        arrange_here(*sizes, scratch[2], data_ref, scratch[1])

    degree = lax.broadcasted_iota(jnp.int32, (half, KTILE), 1)
    parity = (1 - 2 * (degree % 2)).astype(jnp.float32)

    def enter(slot, carry):
        by_count(slot, lambda copy: copy.wait())

        @pl.when(slot - begin >= stages)
        def _():
            put(slot - stages).wait()

        def clear(tile, carry):
            cols = pl.ds(pl.multiple_of(tile * KTILE, KTILE), KTILE)
            staged[lax.rem(slot, stages), :, :, cols] = jnp.zeros((2, levels, KTILE), jnp.float32)
            return carry

        lax.fori_loop(tile_count(slot), tiles, clear, 0)
        return carry

    def leave(slot, carry):
        put(slot).start()
        return carry

    def one_tile(item):
        slot, tile = slot_of[item], tile_of[item]
        place, stage = lax.rem(slot, buffers), lax.rem(slot, stages)
        cols = pl.ds(pl.multiple_of(tile * KTILE, KTILE), KTILE)
        product = lax.dot_general(
            data_ref[slot],
            held[place, cols, :],
            (((1,), (1,)), ((), ())),
            preferred_element_type=jnp.float32,
        )
        both = product[:half] + parity * product[half:]
        both = jnp.where(degree < limit_ref[slot] - tile * KTILE, both, 0.0)
        for c in range(2):
            staged[stage, c, :, cols] = both[c * levels : (c + 1) * levels]

    def one_group(group, carry):
        fetched, entered, left = carry
        item = group * GROUP
        newest = slot_of[item + GROUP - 1]
        wanted = jnp.minimum(slot_of[item] + buffers, end)
        lax.fori_loop(fetched, wanted, start, 0)
        lax.fori_loop(entered, newest + 1, enter, 0)
        for i in range(GROUP):
            one_tile(item + i)
        done = jnp.where(last_of[newest - begin] <= item + GROUP, newest + 1, newest)
        lax.fori_loop(left, done, leave, 0)
        return jnp.maximum(fetched, wanted), newest + 1, done

    groups = lax.div(total + GROUP - 1, GROUP)
    lax.fori_loop(0, groups, one_group, (min(begin + buffers, end), begin, begin))
    for slot in range(max(begin, end - stages), end):
        put(slot).wait()


def legendre_sum(limits, moved, table, level, levels, total_levels, lat_size, lon_size, before):
    slots, degrees, lats = table.shape
    tiles = degrees // KTILE
    anywhere = pl.BlockSpec(memory_space=pl.ANY)
    here = moved.shape[2] == LANES and levels == 8
    if not here:
        moved = arrange(moved, slots, lat_size, lon_size)
    operands = [limits, moved, table] + ([] if before is None else [before])
    items = slots * tiles + GROUP
    data = [pltpu.VMEM((slots, 4 * levels, lats), jnp.bfloat16)]
    if here:
        data.append(pltpu.VMEM((lat_size, slots * 2 * levels, LANES), jnp.float32))
        data.append(pltpu.VMEM(moved.shape, jnp.bfloat16))
    return pl.pallas_call(
        functools.partial(
            legendre_kernel, tiles, level, (lat_size, lon_size) if here else None, before is not None
        ),
        out_shape=jax.ShapeDtypeStruct((slots, 2, total_levels, degrees), jnp.float32),
        in_specs=[pl.BlockSpec(memory_space=pltpu.SMEM)] + [anywhere] * (2 if before is None else 3),
        out_specs=anywhere,
        scratch_shapes=[
            pltpu.VMEM((BUFFERS, degrees, lats), jnp.bfloat16),
            pltpu.VMEM((GROUP, 2, levels, degrees), jnp.float32),
            pltpu.SMEM((items,), jnp.int32),
            pltpu.SMEM((items,), jnp.int32),
            pltpu.SMEM((slots,), jnp.int32),
            pltpu.SemaphoreType.DMA((BUFFERS,)),
            pltpu.SemaphoreType.DMA((GROUP,)),
        ]
        + data
        + [pltpu.SemaphoreType.DMA],
        input_output_aliases={} if before is None else {3: 0},
        compiler_params=pltpu.CompilerParams(vmem_limit_bytes=VMEM),
        cost_estimate=pl.CostEstimate(
            flops=slots * degrees * lats * 4 * levels,
            bytes_accessed=slots * degrees * (lats + 8 * levels),
            transcendentals=0,
        ),
        name="legendre_sum",
    )(*operands)


def after(value, earlier):
    return value if earlier is None else lax.optimization_barrier((value, earlier))[0]


def spread(vorticity, chunk, lon_size, hop_order):
    hemis, lats, part = vorticity.shape[1:]
    me = lax.axis_index("lon")

    def piece(distance, source):
        level = chunk * lon_size + (me ^ distance)
        block = lax.dynamic_index_in_dim(source, level, 0, keepdims=False) * PRESCALE
        return block.astype(jnp.float16).reshape(hemis * lats, part)

    got, source, rounded = {}, vorticity, None
    for turn, distance in enumerate(hop_order):
        if turn in (1, 3):
            source = after(source, rounded)
        rounded = piece(distance, source)
        got[distance] = lax.ppermute(rounded, "lon", [(i, i ^ distance) for i in range(lon_size)])
    got[0] = piece(0, source)
    return got


def spread_whole(vorticity, chunk, lon_size, earlier):
    hemis, lats, part = vorticity.shape[1:]
    block = vorticity[chunk * lon_size : (chunk + 1) * lon_size] * PRESCALE
    block = after(block.astype(jnp.float16).reshape(lon_size, hemis * lats, part), earlier)
    return lax.all_to_all(block, "lon", split_axis=0, concat_axis=0, tiled=True)


def on_device(lat_size, lon_size, high, low, vorticity, legendre, wave_order):
    levels, hemis, lats, part = vorticity.shape
    slot_count = legendre.shape[0]
    devices = lat_size * lon_size
    waves = wave_order.astype(jnp.int32)
    lower, upper = waves % FIRST, waves // FIRST
    near = lower < HALF
    index = jnp.where(near, lower, FIRST - lower) * ROWS_K + jnp.where(near, 0, 2 * KEEP) + 2 * upper
    first_slot = lax.axis_index(("lat", "lon")) * slot_count
    limits = waves.shape[0] - lax.dynamic_slice_in_dim(waves, first_slot, slot_count)
    me = lax.axis_index("lon").reshape(1)
    chunks = levels // lon_size
    hop_order = sorted(range(1, lon_size), key=lambda d: (-(d >> 1), d & 1))

    got = spread(vorticity, 0, lon_size, hop_order)
    circles = [jnp.stack([got[i].astype(jnp.float32) for i in range(lon_size)])]
    for chunk in range(1, chunks):
        circles.append(spread_whole(vorticity, chunk, lon_size, tuple(got[d] for d in hop_order)).astype(jnp.float32))
    done = None
    moved = []
    for chunk in range(chunks):
        origin = me if chunk == 0 else jnp.zeros_like(me)
        chosen = fourier_slots(after(circles[chunk], done), origin, index, high, low)
        done = chosen
        chosen = chosen.reshape(devices, slot_count * 2, hemis * lats)
        moved.append(lax.all_to_all(chosen, ("lat", "lon"), split_axis=0, concat_axis=0, tiled=True))
    result = None
    for chunk in range(chunks):
        first = chunk * lon_size
        result = legendre_sum(limits, moved[chunk], legendre, first, lon_size, levels, lat_size, lon_size, result)
    return result


def solution(mesh):
    lat_size, lon_size = mesh.shape["lat"], mesh.shape["lon"]

    def whole(vorticity, legendre, wave_order):
        high, low = second_tables(vorticity.shape[3])
        body = functools.partial(on_device, lat_size, lon_size, high, low)
        return jax.shard_map(
            body,
            mesh=mesh,
            in_specs=(P(None, None, "lat", "lon"), P(("lat", "lon"), None, None), P()),
            out_specs=P(("lat", "lon"), None, None, None),
            check_vma=False,
        )(vorticity, legendre, wave_order)

    return whole
```

time: 199 us -> 194 us (0.975)
  blocking collectives: 19.7 us -> 0 us
  Pallas kernels: 70.3 us -> 84 us
    all_to_all x1 -> x0, blocking collectives: 19.7 us -> none  [on_device(): lax.all_to_all(chosen, ('lat', 'lon'), split_axis=0, concat_axis=0, tiled...]
    pallas_call x7 -> x4, Pallas kernels: 70.3 us -> 84 us  [the longest x2 50.2 us: legendre_sum(): pl.pallas_call(functools.partial(legendre_kernel, tiles, level, (lat_size...]
    all_to_all x2, waiting for transfers between devices: 7.38 us -> 9.97 us  [on_device(): lax.all_to_all(chosen, ('lat', 'lon'), split_axis=0, concat_axis=0, tiled...]
    ppermute x7, waiting for transfers between devices: 12.9 us -> 10.8 us  [spread(): lax.ppermute(rounded, 'lon', [(i, i ^ distance) for i in range(lon_size)])]
    convert_element_type x1 -> x3, other arithmetic: 2.72 us -> 4.41 us  [piece(): return block.astype(jnp.float16).reshape(hemis * lats, part)]
    unnamed x15 -> x17, local copies, waits for them, and re-layouts: 4 us -> 5.56 us
  transfers between devices with their start and end apart: 10 -> 10, of which waited for: 5 -> 5; matrix products, arithmetic and copies ran while one was open for 7% -> 9% of each run, Pallas kernels for 27% -> 30%
where the time goes in v3:
time: 194 us; the launch traced here: 193 us
  Pallas kernels  84 us (43%)
  waiting for transfers between devices  45.2 us (23%)
  starting transfers between devices  43.3 us (22%)
  other arithmetic  14.8 us (8%)
  local copies, waits for them, and re-layouts  5.61 us (3%)
    pallas_call x2, Pallas kernels, legendre_sum(): pl.pallas_call(functools.partial(legendre_kernel, tiles, level, (lat_size...  50.2 us
    pallas_call x2, Pallas kernels, fourier_slots(): pl.pallas_call(functools.partial(fourier_kernel, rows, slots), out_shape=...  33.8 us
    ppermute x7, starting transfers between devices, spread(): lax.ppermute(rounded, 'lon', [(i, i ^ distance) for i in range(lon_size)])  33.3 us
    all_to_all x1, waiting for transfers between devices, spread_whole(): return lax.all_to_all(block, 'lon', split_axis=0, concat_axis=0, tiled=True)  24.4 us
    ppermute x7, waiting for transfers between devices, spread(): lax.ppermute(rounded, 'lon', [(i, i ^ distance) for i in range(lon_size)])  10.8 us
    all_to_all x2, waiting for transfers between devices, on_device(): lax.all_to_all(chosen, ('lat', 'lon'), split_axis=0, concat_axis=0, tiled...  9.97 us
    all_to_all x2, starting transfers between devices, on_device(): lax.all_to_all(chosen, ('lat', 'lon'), split_axis=0, concat_axis=0, tiled...  6.28 us
    unnamed x17, local copies, waits for them, and re-layouts  5.56 us
  transfers between devices with their start and end apart: 10, of which 5 were waited for; matrix products, arithmetic and copies ran while one was open for 9% of the time, Pallas kernels for 30%

profile of v3, /device:TPU:0, one launch (start us, length us, event | category | flops | bytes accessed | tf_op | source)
XLA Modules:
  0.0 193.2 jit_solution(2042174521165373292)
XLA Ops:
  0.0 1.1 multiply_convert_fusion.8
  1.1 5.1 %collective-permute-start = (f16[128,1024]{1,0:T(8,128)(2,1)S(1)}, f16[128,1024]{1,0:T(8,128)(2,1)S(1)}, u32[]{:S(2)}, u32[]{:S(2)}) collective-permute-start(f16[128,1024]{1,0:T(8,128)(2,1)S(1)} %bitcast.29), channel_id=1, source_target_pairs={{0,6},{1,7},{2,4},{3,5},{4,2},{5,3},{6,0},{7,1},{8,14},{9,15},{10,... | collective-permute-start | bytes 786440 | tf_op jit(solution)/shard_map/ppermute | solution.py:395
  6.2 1.3 multiply_convert_fusion.6
  7.5 1.2 collective-permute-start.1
  8.8 0.8 collective-permute-start.2
  9.5 2.0 %multiply_convert_fusion.1 = (f16[1,2,64,1024]{3,2,1,0:T(8,128)(2,1)S(1)}, f16[1,2,64,1024]{3,2,1,0:T(8,128)(2,1)S(1)}, f16[1,2,64,1024]{3,2,1,0:T(8,128)(2,1)S(...) fusion(f32[16,2,64,1024]{3,2,1,0:T(8,128)} %param.5, s32[]{:T(128)S(6)} %select_n.59, s32[]{:T(128)S(6)} %select_n.58, ...), kind=kLoop, calls=%fused_computation.1 | loop fusion | flops 1310720 | bytes 3932180 | tf_op jit(solution)/shard_map/convert_element_type | solution.py:388
  11.6 0.6 collective-permute-start.6
  12.2 4.3 %collective-permute-start.5 = (f16[128,1024]{1,0:T(8,128)(2,1)S(1)}, f16[128,1024]{1,0:T(8,128)(2,1)S(1)}, u32[]{:S(2)}, u32[]{:S(2)}) collective-permute-start(f16[128,1024]{1,0:T(8,128)(2,1)S(1)} %bitcast.34), channel_id=1, source_target_pairs={{0,3},{1,2},{2,1},{3,0},{4,7},{5,6},{6,5},{7,4},{8,11},{9,10},{10,... | collective-permute-start | bytes 786440 | tf_op jit(solution)/shard_map/ppermute | solution.py:395
  16.5 0.0 collective-permute-done
  16.5 13.6 %collective-permute-start.4 = (f16[128,1024]{1,0:T(8,128)(2,1)S(1)}, f16[128,1024]{1,0:T(8,128)(2,1)S(1)}, u32[]{:S(2)}, u32[]{:S(2)}) collective-permute-start(f16[128,1024]{1,0:T(8,128)(2,1)S(1)} %bitcast.33), channel_id=1, source_target_pairs={{0,2},{1,3},{2,0},{3,1},{4,6},{5,7},{6,4},{7,5},{8,10},{9,11},{10,... | collective-permute-start | bytes 786440 | tf_op jit(solution)/shard_map/ppermute | solution.py:395
  30.0 0.0 collective-permute-done.1
  30.0 7.7 %collective-permute-start.3 = (f16[128,1024]{1,0:T(8,128)(2,1)S(1)}, f16[128,1024]{1,0:T(8,128)(2,1)}, u32[]{:S(2)}, u32[]{:S(2)}) collective-permute-start(f16[128,1024]{1,0:T(8,128)(2,1)S(1)} %bitcast.32), channel_id=1, source_target_pairs={{0,5},{1,4},{2,7},{3,6},{4,1},{5,0},{6,3},{7,2},{8,13},{9,12},{10,... | collective-permute-start | bytes 786440 | tf_op jit(solution)/shard_map/ppermute | solution.py:395
  37.8 4.1 %multiply_convert_fusion = f16[8,2,64,1024]{3,2,1,0:T(8,128)(2,1)} fusion(f32[16,2,64,1024]{3,2,1,0:T(8,128)} %param.5), kind=kLoop, calls=%fused_computation | loop fusion | flops 2097152 | bytes 6291456 | tf_op jit(solution)/shard_map/convert_element_type | solution.py:403
  41.9 6.5 %collective-permute-done.2 = f16[128,1024]{1,0:T(8,128)(2,1)S(1)} collective-permute-done((f16[128,1024]{1,0:T(8,128)(2,1)S(1)}, f16[128,1024]{1,0:T(8,128)(2,1)S(1)}, u32[]{:S(2)}, u32[]{:S(2)}) %collective-permute-start.2) | collective-permute-done | bytes 262176 | tf_op jit(solution)/shard_map/ppermute | solution.py:395
  48.4 0.0 collective-permute-done.6
  48.4 0.0 copy-start.2
  48.4 0.0 collective-permute-done.5
  48.4 0.7 copy-done.2
  49.1 0.0 collective-permute-done.4
  49.1 0.0 copy-start.3
  49.1 0.7 copy-done.3
  49.8 4.3 %collective-permute-done.3 = f16[128,1024]{1,0:T(8,128)(2,1)} collective-permute-done((f16[128,1024]{1,0:T(8,128)(2,1)S(1)}, f16[128,1024]{1,0:T(8,128)(2,1)}, u32[]{:S(2)}, u32[]{:S(2)}) %collective-permute-start.3) | collective-permute-done | bytes 262176 | tf_op jit(solution)/shard_map/ppermute | solution.py:395
  54.1 0.0 copy-start.4
  54.1 3.7 %all-to-all-start = ((f16[8,128,1024]{2,1,0:T(8,128)(2,1)}), f16[8,128,1024]{2,1,0:T(8,128)(2,1)S(1)}, u32[]{:S(2)}, u32[]{:S(2)}) async-start(f16[8,128,1024]{2,1,0:T(8,128)(2,1)} %bitcast), calls=%async_computation | async-start | bytes 4194304 | tf_op jit(solution)/shard_map/all_to_all | solution.py:404
  57.9 0.0 copy-done.4
  57.9 0.6 fusion.1.index_ref
  58.5 1.0 bitcast_dynamic-update-slice_fusion.6
  59.5 1.0 bitcast_dynamic-update-slice_fusion.5
  60.6 1.0 bitcast_dynamic-update-slice_fusion.2
  61.8 2.5 %stack.42.x_ref = f32[8,128,1024]{2,1,0:T(8,128)} convert(f16[8,128,1024]{2,1,0:T(8,128)(2,1)S(1)} %bitcast_dynamic-update-slice_fusion) | non-fusion elementwise | flops 1048576 | bytes 6291456 | tf_op jit(solution)/shard_map/stack | solution.py:422
  64.3 16.9 %fourier_slots.2 = bf16[4096,128]{1,0:T(8,128)(2,1)} custom-call(s32[2048]{0:T(1024)} %fusion.1.index_ref, s32[1]{0:T(128)} %bitcast.8.me_ref, f32[8,128,1024]{2,1,0:T(8,128)} %stack.42.x_ref, bf16[33,128,256]{2,1,0:T(8,128)(2,1)} %constant.88.clone.high_ref, bf16[33,128,256]{2,1,0:T(8,128)(2,1)} %constant.89.clone.low_ref), custom_call_target="tpu_custom_call" | custom-call | flops 830472192 | bytes 12582912 | tf_op jit(solution)/shard_map/fourier_slots/pallas_call | solution.py:171
  81.2 24.4 %all-to-all-done = f16[8,128,1024]{2,1,0:T(8,128)(2,1)S(1)} async-done(((f16[8,128,1024]{2,1,0:T(8,128)(2,1)}), f16[8,128,1024]{2,1,0:T(8,128)(2,1)S(1)}, u32[]{:S(2)}, u32[]{:S(2)}) %all-to-all-start) | async-done | bytes 2097184 | tf_op jit(solution)/shard_map/all_to_all | solution.py:404
  105.6 3.6 %all-to-all-start.2 = ((bf16[32,128,128]{2,1,0:T(8,128)(2,1)}), bf16[32,128,128]{2,1,0:T(8,128)(2,1)S(1)}, u32[]{:S(2)}, u32[]{:S(2)}) async-start(bf16[32,128,128]{2,1,0:T(8,128)(2,1)} %bitcast.27), calls=%async_computation.2 | async-start | bytes 2097152 | tf_op jit(solution)/shard_map/all_to_all | solution.py:432
  109.2 2.5 %convert_element_type.100.x_ref = f32[8,128,1024]{2,1,0:T(8,128)} convert(f16[8,128,1024]{2,1,0:T(8,128)(2,1)S(1)} %all-to-all-done) | non-fusion elementwise | flops 1048576 | bytes 6291456 | tf_op jit(solution)/shard_map/convert_element_type | solution.py:424
  111.8 16.9 %fourier_slots.3 = bf16[4096,128]{1,0:T(8,128)(2,1)} custom-call(s32[2048]{0:T(1024)} %fusion.1.index_ref, s32[1]{0:T(128)} %constant.81.clone.1.me_ref, f32[8,128,1024]{2,1,0:T(8,128)} %convert_element_type.100.x_ref, bf16[33,128,256]{2,1,0:T(8,128)(2,1)} %constant.88.clone.high_ref, bf16[33,128,256]{2,1,0:T(8,128)(2,1)} %constant.89.clone.low_ref), custom_call_target="tpu_custom_call" | custom-call | flops 830472192 | bytes 12582912 | tf_op jit(solution)/shard_map/fourier_slots/pallas_call | solution.py:171
  128.7 8.2 %all-to-all-done.2.moved_ref = bf16[32,128,128]{2,1,0:T(8,128)(2,1)S(1)} async-done(((bf16[32,128,128]{2,1,0:T(8,128)(2,1)}), bf16[32,128,128]{2,1,0:T(8,128)(2,1)S(1)}, u32[]{:S(2)}, u32[]{:S(2)}) %all-to-all-start.2) | async-done | bytes 1048608 | tf_op jit(solution)/shard_map/all_to_all | solution.py:432
  136.8 0.0 copy-start
  136.8 2.6 %all-to-all-start.1 = ((bf16[32,128,128]{2,1,0:T(8,128)(2,1)}), bf16[32,128,128]{2,1,0:T(8,128)(2,1)S(1)}, u32[]{:S(2)}, u32[]{:S(2)}) async-start(bf16[32,128,128]{2,1,0:T(8,128)(2,1)} %bitcast.26), calls=%async_computation.1 | async-start | bytes 2097152 | tf_op jit(solution)/shard_map/all_to_all | solution.py:432
  139.5 0.7 dynamic-slice_subtract_fusion.limit_ref
  140.2 0.0 copy-done
  140.2 25.1 %legendre_sum.2.refs_0_ = f32[64,2,16,2048]{3,2,1,0:T(8,128)} custom-call(s32[64]{0:T(128)} %dynamic-slice_subtract_fusion.limit_ref, bf16[32,128,128]{2,1,0:T(8,128)(2,1)} %copy-done, bf16[64,2048,256]{2,1,0:T(8,128)(2,1)} %table_ref.3), custom_call_target="tpu_custom_call" | custom-call | flops 1073741824 | bytes 41943040 | tf_op jit(solution)/shard_map/legendre_sum/pallas_call | solution.py:348
  165.3 1.8 all-to-all-done.1.moved_ref
  167.1 0.0 copy-start.1
  167.1 1.0 copy-done.1
  168.1 25.1 %legendre_sum.3 = f32[64,2,16,2048]{3,2,1,0:T(8,128)} custom-call(s32[64]{0:T(128)} %dynamic-slice_subtract_fusion.limit_ref, bf16[32,128,128]{2,1,0:T(8,128)(2,1)} %copy-done.1, bf16[64,2048,256]{2,1,0:T(8,128)(2,1)} %table_ref.3, f32[64,2,16,2048]{3,2,1,0:T(8,128)} %legendre_sum.2.refs_0_), custom_call_target="tpu_custom_call", output_to_operand_aliasing={{}: (3, {})} | custom-call | flops 1073741824 | bytes 41943040 | tf_op jit(solution)/shard_map/legendre_sum/pallas_call | solution.py:348
  (5 shorter events, 0.2 us)
Async XLA Ops:
  1.1 15.4 %collective-permute-start = (f16[128,1024]{1,0:T(8,128)(2,1)S(1)}, f16[128,1024]{1,0:T(8,128)(2,1)S(1)}, u32[]{:S(2)}, u32[]{:S(2)}) collective-permute-start(f16[128,1024]{1,0:T(8,128)(2,1)S(1)} %bitcast.29), channel_id=1, source_target_pairs={{0,6},{1,7},{2,4},{3,5},{4,2},{5,3},{6,0},{7,1},{8,14},{9,15},{10,... | collective-permute-start | bytes 786440 | tf_op jit(solution)/shard_map/ppermute | solution.py:395
  7.5 22.5 %collective-permute-start.1 = (f16[128,1024]{1,0:T(8,128)(2,1)S(1)}, f16[128,1024]{1,0:T(8,128)(2,1)S(1)}, u32[]{:S(2)}, u32[]{:S(2)}) collective-permute-start(f16[128,1024]{1,0:T(8,128)(2,1)S(1)} %bitcast.31), channel_id=1, source_target_pairs={{0,7},{1,6},{2,5},{3,4},{4,3},{5,2},{6,1},{7,0},{8,15},{9,14},{10,... | collective-permute-start | bytes 786440 | tf_op jit(solution)/shard_map/ppermute | solution.py:395
  8.8 39.7 %collective-permute-start.2 = (f16[128,1024]{1,0:T(8,128)(2,1)S(1)}, f16[128,1024]{1,0:T(8,128)(2,1)S(1)}, u32[]{:S(2)}, u32[]{:S(2)}) collective-permute-start(f16[128,1024]{1,0:T(8,128)(2,1)S(1)} %bitcast.30), channel_id=1, source_target_pairs={{0,4},{1,5},{2,6},{3,7},{4,0},{5,1},{6,2},{7,3},{8,12},{9,13},{10,... | collective-permute-start | bytes 786440 | tf_op jit(solution)/shard_map/ppermute | solution.py:395
  11.6 36.9 %collective-permute-start.6 = (f16[128,1024]{1,0:T(8,128)(2,1)S(1)}, f16[128,1024]{1,0:T(8,128)(2,1)S(1)}, u32[]{:S(2)}, u32[]{:S(2)}) collective-permute-start(f16[128,1024]{1,0:T(8,128)(2,1)S(1)} %bitcast.35), channel_id=1, source_target_pairs={{0,1},{1,0},{2,3},{3,2},{4,5},{5,4},{6,7},{7,6},{8,9},{9,8},{10,11... | collective-permute-start | bytes 786440 | tf_op jit(solution)/shard_map/ppermute | solution.py:395
  12.2 36.3 %collective-permute-start.5 = (f16[128,1024]{1,0:T(8,128)(2,1)S(1)}, f16[128,1024]{1,0:T(8,128)(2,1)S(1)}, u32[]{:S(2)}, u32[]{:S(2)}) collective-permute-start(f16[128,1024]{1,0:T(8,128)(2,1)S(1)} %bitcast.34), channel_id=1, source_target_pairs={{0,3},{1,2},{2,1},{3,0},{4,7},{5,6},{6,5},{7,4},{8,11},{9,10},{10,... | collective-permute-start | bytes 786440 | tf_op jit(solution)/shard_map/ppermute | solution.py:395
  16.5 32.7 %collective-permute-start.4 = (f16[128,1024]{1,0:T(8,128)(2,1)S(1)}, f16[128,1024]{1,0:T(8,128)(2,1)S(1)}, u32[]{:S(2)}, u32[]{:S(2)}) collective-permute-start(f16[128,1024]{1,0:T(8,128)(2,1)S(1)} %bitcast.33), channel_id=1, source_target_pairs={{0,2},{1,3},{2,0},{3,1},{4,6},{5,7},{6,4},{7,5},{8,10},{9,11},{10,... | collective-permute-start | bytes 786440 | tf_op jit(solution)/shard_map/ppermute | solution.py:395
  30.0 24.1 %collective-permute-start.3 = (f16[128,1024]{1,0:T(8,128)(2,1)S(1)}, f16[128,1024]{1,0:T(8,128)(2,1)}, u32[]{:S(2)}, u32[]{:S(2)}) collective-permute-start(f16[128,1024]{1,0:T(8,128)(2,1)S(1)} %bitcast.32), channel_id=1, source_target_pairs={{0,5},{1,4},{2,7},{3,6},{4,1},{5,0},{6,3},{7,2},{8,13},{9,12},{10,... | collective-permute-start | bytes 786440 | tf_op jit(solution)/shard_map/ppermute | solution.py:395
  48.4 0.7 copy-start.2
  49.1 0.7 copy-start.3
  54.1 3.8 %copy-start.4 = (s32[2048]{0:T(1024)S(1)}, s32[2048]{0:T(1024)}, u32[]{:S(2)}) copy-start(s32[2048]{0:T(1024)} %param.7) | copy-start | bytes 24580
  54.1 51.5 %all-to-all-start = ((f16[8,128,1024]{2,1,0:T(8,128)(2,1)}), f16[8,128,1024]{2,1,0:T(8,128)(2,1)S(1)}, u32[]{:S(2)}, u32[]{:S(2)}) async-start(f16[8,128,1024]{2,1,0:T(8,128)(2,1)} %bitcast), calls=%async_computation | async-start | bytes 4194304 | tf_op jit(solution)/shard_map/all_to_all | solution.py:404
  105.6 31.2 %all-to-all-start.2 = ((bf16[32,128,128]{2,1,0:T(8,128)(2,1)}), bf16[32,128,128]{2,1,0:T(8,128)(2,1)S(1)}, u32[]{:S(2)}, u32[]{:S(2)}) async-start(bf16[32,128,128]{2,1,0:T(8,128)(2,1)} %bitcast.27), calls=%async_computation.2 | async-start | bytes 2097152 | tf_op jit(solution)/shard_map/all_to_all | solution.py:432
  136.8 3.3 %copy-start = (bf16[32,128,128]{2,1,0:T(8,128)(2,1)}, bf16[32,128,128]{2,1,0:T(8,128)(2,1)S(1)}, u32[]{:S(2)}) copy-start(bf16[32,128,128]{2,1,0:T(8,128)(2,1)S(1)} %all-to-all-done.2.moved_ref) | copy-start | bytes 3145732
  136.8 30.2 %all-to-all-start.1 = ((bf16[32,128,128]{2,1,0:T(8,128)(2,1)}), bf16[32,128,128]{2,1,0:T(8,128)(2,1)S(1)}, u32[]{:S(2)}, u32[]{:S(2)}) async-start(bf16[32,128,128]{2,1,0:T(8,128)(2,1)} %bitcast.26), calls=%async_computation.1 | async-start | bytes 2097152 | tf_op jit(solution)/shard_map/all_to_all | solution.py:432
  167.1 1.0 copy-start.1

commit v4 on v3

--- a/solution.py
+++ b/solution.py
@@ -416,7 +416,7 @@
     limits = waves.shape[0] - lax.dynamic_slice_in_dim(waves, first_slot, slot_count)
     me = lax.axis_index("lon").reshape(1)
     chunks = levels // lon_size
-    hop_order = sorted(range(1, lon_size), key=lambda d: (-(d >> 1), d & 1))
+    hop_order = sorted(range(1, lon_size), key=lambda d: (d & 1, -(d >> 1)))
 
     got = spread(vorticity, 0, lon_size, hop_order)
     circles = [jnp.stack([got[i].astype(jnp.float32) for i in range(lon_size)])]

time: 194 us -> 191 us (0.985)
  starting transfers between devices: 43.3 us -> 38.2 us
  waiting for transfers between devices: 45.2 us -> 49 us
    ppermute x7, starting transfers between devices: 33.3 us -> 24.9 us  [spread(): lax.ppermute(rounded, 'lon', [(i, i ^ distance) for i in range(lon_size)])]
    all_to_all x1, starting transfers between devices: 3.73 us -> 6.93 us  [spread_whole(): return lax.all_to_all(block, 'lon', split_axis=0, concat_axis=0, tiled=True)]
    ppermute x7, waiting for transfers between devices: 10.8 us -> 13.1 us  [spread(): lax.ppermute(rounded, 'lon', [(i, i ^ distance) for i in range(lon_size)])]
    unnamed x17 -> x23, local copies, waits for them, and re-layouts: 5.56 us -> 4.39 us
  transfers between devices with their start and end apart: 10 -> 10, of which waited for: 5 -> 6; matrix products, arithmetic and copies ran while one was open for 9% -> 8% of each run, Pallas kernels for 30% -> 31%
where the time goes in v4:
time: 191 us
  Pallas kernels  84.1 us (44%)
  waiting for transfers between devices  49 us (26%)
  starting transfers between devices  38.2 us (20%)
  other arithmetic  14.8 us (8%)
  local copies, waits for them, and re-layouts  4.44 us (2%)
    pallas_call x2, Pallas kernels, legendre_sum(): pl.pallas_call(functools.partial(legendre_kernel, tiles, level, (lat_size...  50.3 us
    pallas_call x2, Pallas kernels, fourier_slots(): pl.pallas_call(functools.partial(fourier_kernel, rows, slots), out_shape=...  33.8 us
    all_to_all x1, waiting for transfers between devices, spread_whole(): return lax.all_to_all(block, 'lon', split_axis=0, concat_axis=0, tiled=True)  25.9 us
    ppermute x7, starting transfers between devices, spread(): lax.ppermute(rounded, 'lon', [(i, i ^ distance) for i in range(lon_size)])  24.9 us
    ppermute x7, waiting for transfers between devices, spread(): lax.ppermute(rounded, 'lon', [(i, i ^ distance) for i in range(lon_size)])  13.1 us
    all_to_all x2, waiting for transfers between devices, on_device(): lax.all_to_all(chosen, ('lat', 'lon'), split_axis=0, concat_axis=0, tiled...  9.99 us
    all_to_all x1, starting transfers between devices, spread_whole(): return lax.all_to_all(block, 'lon', split_axis=0, concat_axis=0, tiled=True)  6.93 us
    all_to_all x2, starting transfers between devices, on_device(): lax.all_to_all(chosen, ('lat', 'lon'), split_axis=0, concat_axis=0, tiled...  6.3 us
  transfers between devices with their start and end apart: 10, of which 6 were waited for; matrix products, arithmetic and copies ran while one was open for 8% of the time, Pallas kernels for 31%

profile of v4, /device:TPU:0, one launch (start us, length us, event | category | flops | bytes accessed | tf_op | source)
XLA Modules:
  0.0 190.7 jit_solution(1861854762327625686)
XLA Ops:
  0.0 1.1 multiply_convert_fusion.8
  1.1 5.1 %collective-permute-start = (f16[128,1024]{1,0:T(8,128)(2,1)S(1)}, f16[128,1024]{1,0:T(8,128)(2,1)S(1)}, u32[]{:S(2)}, u32[]{:S(2)}) collective-permute-start(f16[128,1024]{1,0:T(8,128)(2,1)S(1)} %bitcast.29), channel_id=1, source_target_pairs={{0,6},{1,7},{2,4},{3,5},{4,2},{5,3},{6,0},{7,1},{8,14},{9,15},{10,... | collective-permute-start | bytes 786440 | tf_op jit(solution)/shard_map/ppermute | solution.py:395
  6.2 1.3 multiply_convert_fusion.6
  7.5 0.1 collective-permute-start.1
  7.6 0.6 collective-permute-start.2
  8.2 2.0 %multiply_convert_fusion.1 = (f16[1,2,64,1024]{3,2,1,0:T(8,128)(2,1)S(1)}, f16[1,2,64,1024]{3,2,1,0:T(8,128)(2,1)S(1)}, f16[1,2,64,1024]{3,2,1,0:T(8,128)(2,1)S(...) fusion(f32[16,2,64,1024]{3,2,1,0:T(8,128)} %param.5, s32[]{:T(128)S(6)} %select_n.59, s32[]{:T(128)S(6)} %select_n.58, ...), kind=kLoop, calls=%fused_computation.1 | loop fusion | flops 1310720 | bytes 3932180 | tf_op jit(solution)/shard_map/convert_element_type | solution.py:388
  10.2 1.8 collective-permute-start.6
  12.0 1.3 collective-permute-start.5
  13.2 0.2 collective-permute-done
  13.5 13.1 %collective-permute-start.4 = (f16[128,1024]{1,0:T(8,128)(2,1)S(1)}, f16[128,1024]{1,0:T(8,128)(2,1)S(1)}, u32[]{:S(2)}, u32[]{:S(2)}) collective-permute-start(f16[128,1024]{1,0:T(8,128)(2,1)S(1)} %bitcast.33), channel_id=1, source_target_pairs={{0,5},{1,4},{2,7},{3,6},{4,1},{5,0},{6,3},{7,2},{8,13},{9,12},{10,... | collective-permute-start | bytes 786440 | tf_op jit(solution)/shard_map/ppermute | solution.py:395
  26.6 3.8 %collective-permute-done.1 = f16[128,1024]{1,0:T(8,128)(2,1)S(1)} collective-permute-done((f16[128,1024]{1,0:T(8,128)(2,1)S(1)}, f16[128,1024]{1,0:T(8,128)(2,1)S(1)}, u32[]{:S(2)}, u32[]{:S(2)}) %collective-permute-start.1) | collective-permute-done | bytes 262176 | tf_op jit(solution)/shard_map/ppermute | solution.py:395
  30.4 3.0 %collective-permute-start.3 = (f16[128,1024]{1,0:T(8,128)(2,1)S(1)}, f16[128,1024]{1,0:T(8,128)(2,1)S(1)}, u32[]{:S(2)}, u32[]{:S(2)}) collective-permute-start(f16[128,1024]{1,0:T(8,128)(2,1)S(1)} %bitcast.32), channel_id=1, source_target_pairs={{0,7},{1,6},{2,5},{3,4},{4,3},{5,2},{6,1},{7,0},{8,15},{9,14},{10,... | collective-permute-start | bytes 786440 | tf_op jit(solution)/shard_map/ppermute | solution.py:395
  33.4 4.1 %multiply_convert_fusion = f16[8,2,64,1024]{3,2,1,0:T(8,128)(2,1)} fusion(f32[16,2,64,1024]{3,2,1,0:T(8,128)} %param.5), kind=kLoop, calls=%fused_computation | loop fusion | flops 2097152 | bytes 6291456 | tf_op jit(solution)/shard_map/convert_element_type | solution.py:403
  37.5 0.0 collective-permute-done.2
  37.5 0.0 collective-permute-done.6
  37.5 0.0 copy-start.2
  37.5 0.0 collective-permute-done.5
  37.5 0.7 copy-done.2
  38.2 9.1 %collective-permute-done.4 = f16[128,1024]{1,0:T(8,128)(2,1)S(1)} collective-permute-done((f16[128,1024]{1,0:T(8,128)(2,1)S(1)}, f16[128,1024]{1,0:T(8,128)(2,1)S(1)}, u32[]{:S(2)}, u32[]{:S(2)}) %collective-permute-start.4) | collective-permute-done | bytes 262176 | tf_op jit(solution)/shard_map/ppermute | solution.py:395
  47.3 0.0 copy-start.3
  47.3 0.7 copy-done.3
  48.0 0.0 collective-permute-done.3
  48.0 0.0 copy-start.5
  48.0 0.7 copy-done.5
  48.7 0.0 copy-start.7
  48.7 6.9 %all-to-all-start = ((f16[8,128,1024]{2,1,0:T(8,128)(2,1)}), f16[8,128,1024]{2,1,0:T(8,128)(2,1)S(1)}, u32[]{:S(2)}, u32[]{:S(2)}) async-start(f16[8,128,1024]{2,1,0:T(8,128)(2,1)} %bitcast), calls=%async_computation | async-start | bytes 4194304 | tf_op jit(solution)/shard_map/all_to_all | solution.py:404
  55.7 0.0 copy-start.4
  55.7 0.0 copy-start.6
  55.7 0.0 copy-done.7
  55.8 0.6 fusion.1.index_ref
  56.4 1.0 bitcast_dynamic-update-slice_fusion.6
  57.5 0.0 copy-done.4
  57.7 0.0 copy-done.6
  57.7 2.5 %stack.42.x_ref = f32[8,128,1024]{2,1,0:T(8,128)} convert(f16[8,128,1024]{2,1,0:T(8,128)(2,1)S(1)} %bitcast_dynamic-update-slice_fusion) | non-fusion elementwise | flops 1048576 | bytes 6291456 | tf_op jit(solution)/shard_map/stack | solution.py:422
  60.2 16.9 %fourier_slots.2 = bf16[4096,128]{1,0:T(8,128)(2,1)} custom-call(s32[2048]{0:T(1024)} %fusion.1.index_ref, s32[1]{0:T(128)} %bitcast.8.me_ref, f32[8,128,1024]{2,1,0:T(8,128)} %stack.42.x_ref, bf16[33,128,256]{2,1,0:T(8,128)(2,1)} %constant.88.clone.high_ref, bf16[33,128,256]{2,1,0:T(8,128)(2,1)} %constant.89.clone.low_ref), custom_call_target="tpu_custom_call" | custom-call | flops 830472192 | bytes 12582912 | tf_op jit(solution)/shard_map/fourier_slots/pallas_call | solution.py:171
  77.1 25.9 %all-to-all-done = f16[8,128,1024]{2,1,0:T(8,128)(2,1)S(1)} async-done(((f16[8,128,1024]{2,1,0:T(8,128)(2,1)}), f16[8,128,1024]{2,1,0:T(8,128)(2,1)S(1)}, u32[]{:S(2)}, u32[]{:S(2)}) %all-to-all-start) | async-done | bytes 2097184 | tf_op jit(solution)/shard_map/all_to_all | solution.py:404
  103.0 3.7 %all-to-all-start.2 = ((bf16[32,128,128]{2,1,0:T(8,128)(2,1)}), bf16[32,128,128]{2,1,0:T(8,128)(2,1)S(1)}, u32[]{:S(2)}, u32[]{:S(2)}) async-start(bf16[32,128,128]{2,1,0:T(8,128)(2,1)} %bitcast.27), calls=%async_computation.2 | async-start | bytes 2097152 | tf_op jit(solution)/shard_map/all_to_all | solution.py:432
  106.7 2.5 %convert_element_type.100.x_ref = f32[8,128,1024]{2,1,0:T(8,128)} convert(f16[8,128,1024]{2,1,0:T(8,128)(2,1)S(1)} %all-to-all-done) | non-fusion elementwise | flops 1048576 | bytes 6291456 | tf_op jit(solution)/shard_map/convert_element_type | solution.py:424
  109.2 16.9 %fourier_slots.3 = bf16[4096,128]{1,0:T(8,128)(2,1)} custom-call(s32[2048]{0:T(1024)} %fusion.1.index_ref, s32[1]{0:T(128)} %constant.81.clone.1.me_ref, f32[8,128,1024]{2,1,0:T(8,128)} %convert_element_type.100.x_ref, bf16[33,128,256]{2,1,0:T(8,128)(2,1)} %constant.88.clone.high_ref, bf16[33,128,256]{2,1,0:T(8,128)(2,1)} %constant.89.clone.low_ref), custom_call_target="tpu_custom_call" | custom-call | flops 830472192 | bytes 12582912 | tf_op jit(solution)/shard_map/fourier_slots/pallas_call | solution.py:171
  126.1 8.1 %all-to-all-done.2.moved_ref = bf16[32,128,128]{2,1,0:T(8,128)(2,1)S(1)} async-done(((bf16[32,128,128]{2,1,0:T(8,128)(2,1)}), bf16[32,128,128]{2,1,0:T(8,128)(2,1)S(1)}, u32[]{:S(2)}, u32[]{:S(2)}) %all-to-all-start.2) | async-done | bytes 1048608 | tf_op jit(solution)/shard_map/all_to_all | solution.py:432
  134.3 0.0 copy-start
  134.3 2.6 %all-to-all-start.1 = ((bf16[32,128,128]{2,1,0:T(8,128)(2,1)}), bf16[32,128,128]{2,1,0:T(8,128)(2,1)S(1)}, u32[]{:S(2)}, u32[]{:S(2)}) async-start(bf16[32,128,128]{2,1,0:T(8,128)(2,1)} %bitcast.26), calls=%async_computation.1 | async-start | bytes 2097152 | tf_op jit(solution)/shard_map/all_to_all | solution.py:432
  137.0 0.6 dynamic-slice_subtract_fusion.limit_ref
  137.6 0.0 copy-done
  137.6 25.1 %legendre_sum.2.refs_0_ = f32[64,2,16,2048]{3,2,1,0:T(8,128)} custom-call(s32[64]{0:T(128)} %dynamic-slice_subtract_fusion.limit_ref, bf16[32,128,128]{2,1,0:T(8,128)(2,1)} %copy-done, bf16[64,2048,256]{2,1,0:T(8,128)(2,1)} %table_ref.3), custom_call_target="tpu_custom_call" | custom-call | flops 1073741824 | bytes 41943040 | tf_op jit(solution)/shard_map/legendre_sum/pallas_call | solution.py:348
  162.7 1.8 all-to-all-done.1.moved_ref
  164.5 0.0 copy-start.1
  164.5 1.0 copy-done.1
  165.5 25.1 %legendre_sum.3 = f32[64,2,16,2048]{3,2,1,0:T(8,128)} custom-call(s32[64]{0:T(128)} %dynamic-slice_subtract_fusion.limit_ref, bf16[32,128,128]{2,1,0:T(8,128)(2,1)} %copy-done.1, bf16[64,2048,256]{2,1,0:T(8,128)(2,1)} %table_ref.3, f32[64,2,16,2048]{3,2,1,0:T(8,128)} %legendre_sum.2.refs_0_), custom_call_target="tpu_custom_call", output_to_operand_aliasing={{}: (3, {})} | custom-call | flops 1073741824 | bytes 41943040 | tf_op jit(solution)/shard_map/legendre_sum/pallas_call | solution.py:348
  (7 shorter events, 0.3 us)
Async XLA Ops:
  1.1 12.4 %collective-permute-start = (f16[128,1024]{1,0:T(8,128)(2,1)S(1)}, f16[128,1024]{1,0:T(8,128)(2,1)S(1)}, u32[]{:S(2)}, u32[]{:S(2)}) collective-permute-start(f16[128,1024]{1,0:T(8,128)(2,1)S(1)} %bitcast.29), channel_id=1, source_target_pairs={{0,6},{1,7},{2,4},{3,5},{4,2},{5,3},{6,0},{7,1},{8,14},{9,15},{10,... | collective-permute-start | bytes 786440 | tf_op jit(solution)/shard_map/ppermute | solution.py:395
  7.5 22.8 %collective-permute-start.1 = (f16[128,1024]{1,0:T(8,128)(2,1)S(1)}, f16[128,1024]{1,0:T(8,128)(2,1)S(1)}, u32[]{:S(2)}, u32[]{:S(2)}) collective-permute-start(f16[128,1024]{1,0:T(8,128)(2,1)S(1)} %bitcast.31), channel_id=1, source_target_pairs={{0,4},{1,5},{2,6},{3,7},{4,0},{5,1},{6,2},{7,3},{8,12},{9,13},{10,... | collective-permute-start | bytes 786440 | tf_op jit(solution)/shard_map/ppermute | solution.py:395
  7.6 29.9 %collective-permute-start.2 = (f16[128,1024]{1,0:T(8,128)(2,1)S(1)}, f16[128,1024]{1,0:T(8,128)(2,1)S(1)}, u32[]{:S(2)}, u32[]{:S(2)}) collective-permute-start(f16[128,1024]{1,0:T(8,128)(2,1)S(1)} %bitcast.30), channel_id=1, source_target_pairs={{0,2},{1,3},{2,0},{3,1},{4,6},{5,7},{6,4},{7,5},{8,10},{9,11},{10,... | collective-permute-start | bytes 786440 | tf_op jit(solution)/shard_map/ppermute | solution.py:395
  10.2 27.3 %collective-permute-start.6 = (f16[128,1024]{1,0:T(8,128)(2,1)S(1)}, f16[128,1024]{1,0:T(8,128)(2,1)S(1)}, u32[]{:S(2)}, u32[]{:S(2)}) collective-permute-start(f16[128,1024]{1,0:T(8,128)(2,1)S(1)} %bitcast.35), channel_id=1, source_target_pairs={{0,1},{1,0},{2,3},{3,2},{4,5},{5,4},{6,7},{7,6},{8,9},{9,8},{10,11... | collective-permute-start | bytes 786440 | tf_op jit(solution)/shard_map/ppermute | solution.py:395
  12.0 25.5 %collective-permute-start.5 = (f16[128,1024]{1,0:T(8,128)(2,1)S(1)}, f16[128,1024]{1,0:T(8,128)(2,1)S(1)}, u32[]{:S(2)}, u32[]{:S(2)}) collective-permute-start(f16[128,1024]{1,0:T(8,128)(2,1)S(1)} %bitcast.34), channel_id=1, source_target_pairs={{0,3},{1,2},{2,1},{3,0},{4,7},{5,6},{6,5},{7,4},{8,11},{9,10},{10,... | collective-permute-start | bytes 786440 | tf_op jit(solution)/shard_map/ppermute | solution.py:395
  13.5 33.8 %collective-permute-start.4 = (f16[128,1024]{1,0:T(8,128)(2,1)S(1)}, f16[128,1024]{1,0:T(8,128)(2,1)S(1)}, u32[]{:S(2)}, u32[]{:S(2)}) collective-permute-start(f16[128,1024]{1,0:T(8,128)(2,1)S(1)} %bitcast.33), channel_id=1, source_target_pairs={{0,5},{1,4},{2,7},{3,6},{4,1},{5,0},{6,3},{7,2},{8,13},{9,12},{10,... | collective-permute-start | bytes 786440 | tf_op jit(solution)/shard_map/ppermute | solution.py:395
  30.4 17.7 %collective-permute-start.3 = (f16[128,1024]{1,0:T(8,128)(2,1)S(1)}, f16[128,1024]{1,0:T(8,128)(2,1)S(1)}, u32[]{:S(2)}, u32[]{:S(2)}) collective-permute-start(f16[128,1024]{1,0:T(8,128)(2,1)S(1)} %bitcast.32), channel_id=1, source_target_pairs={{0,7},{1,6},{2,5},{3,4},{4,3},{5,2},{6,1},{7,0},{8,15},{9,14},{10,... | collective-permute-start | bytes 786440 | tf_op jit(solution)/shard_map/ppermute | solution.py:395
  37.5 0.7 copy-start.2
  47.3 0.7 copy-start.3
  48.0 0.7 copy-start.5
  48.7 7.0 %copy-start.7 = (s32[2048]{0:T(1024)S(1)}, s32[2048]{0:T(1024)}, u32[]{:S(2)}) copy-start(s32[2048]{0:T(1024)} %param.7) | copy-start | bytes 24580
  48.7 54.3 %all-to-all-start = ((f16[8,128,1024]{2,1,0:T(8,128)(2,1)}), f16[8,128,1024]{2,1,0:T(8,128)(2,1)S(1)}, u32[]{:S(2)}, u32[]{:S(2)}) async-start(f16[8,128,1024]{2,1,0:T(8,128)(2,1)} %bitcast), calls=%async_computation | async-start | bytes 4194304 | tf_op jit(solution)/shard_map/all_to_all | solution.py:404
  55.7 1.9 copy-start.4
  55.7 2.0 %copy-start.6 = (f16[128,1024]{1,0:T(8,128)(2,1)S(1)}, f16[128,1024]{1,0:T(8,128)(2,1)}, u32[]{:S(2)}) copy-start(f16[128,1024]{1,0:T(8,128)(2,1)} %copy-done.5) | copy-start | bytes 786436
  103.0 31.2 %all-to-all-start.2 = ((bf16[32,128,128]{2,1,0:T(8,128)(2,1)}), bf16[32,128,128]{2,1,0:T(8,128)(2,1)S(1)}, u32[]{:S(2)}, u32[]{:S(2)}) async-start(bf16[32,128,128]{2,1,0:T(8,128)(2,1)} %bitcast.27), calls=%async_computation.2 | async-start | bytes 2097152 | tf_op jit(solution)/shard_map/all_to_all | solution.py:432
  134.3 3.3 %copy-start = (bf16[32,128,128]{2,1,0:T(8,128)(2,1)}, bf16[32,128,128]{2,1,0:T(8,128)(2,1)S(1)}, u32[]{:S(2)}) copy-start(bf16[32,128,128]{2,1,0:T(8,128)(2,1)S(1)} %all-to-all-done.2.moved_ref) | copy-start | bytes 3145732
  134.3 30.2 %all-to-all-start.1 = ((bf16[32,128,128]{2,1,0:T(8,128)(2,1)}), bf16[32,128,128]{2,1,0:T(8,128)(2,1)S(1)}, u32[]{:S(2)}, u32[]{:S(2)}) async-start(bf16[32,128,128]{2,1,0:T(8,128)(2,1)} %bitcast.26), calls=%async_computation.1 | async-start | bytes 2097152 | tf_op jit(solution)/shard_map/all_to_all | solution.py:432
  164.5 1.0 copy-start.1

commit v5 on v4

--- a/solution.py
+++ b/solution.py
@@ -389,7 +389,7 @@
 
     got, source, rounded = {}, vorticity, None
     for turn, distance in enumerate(hop_order):
-        if turn in (1, 3):
+        if turn == 1:
             source = after(source, rounded)
         rounded = piece(distance, source)
         got[distance] = lax.ppermute(rounded, "lon", [(i, i ^ distance) for i in range(lon_size)])

time: 191 us -> 191 us (level)
  waiting for transfers between devices: 49 us -> 60.3 us
  starting transfers between devices: 38.2 us -> 28.5 us
    ppermute x7, waiting for transfers between devices: 13.1 us -> 25.2 us  [spread(): lax.ppermute(rounded, 'lon', [(i, i ^ distance) for i in range(lon_size)])]
    ppermute x7, starting transfers between devices: 24.9 us -> 17.4 us  [spread(): lax.ppermute(rounded, 'lon', [(i, i ^ distance) for i in range(lon_size)])]
    all_to_all x1, starting transfers between devices: 6.93 us -> 4.84 us  [spread_whole(): return lax.all_to_all(block, 'lon', split_axis=0, concat_axis=0, tiled=True)]
    convert_element_type x3 -> x2, other arithmetic: 4.41 us -> 3.58 us  [piece(): return block.astype(jnp.float16).reshape(hemis * lats, part)]
    unnamed x23 -> x21, local copies, waits for them, and re-layouts: 4.39 us -> 4.63 us
where the time goes in v5:
time: 191 us
  Pallas kernels  83.9 us (44%)
  waiting for transfers between devices  60.3 us (32%)
  starting transfers between devices  28.5 us (15%)
  other arithmetic  13.9 us (7%)
  local copies, waits for them, and re-layouts  4.68 us (2%)
    pallas_call x2, Pallas kernels, legendre_sum(): pl.pallas_call(functools.partial(legendre_kernel, tiles, level, (lat_size...  50.1 us
    pallas_call x2, Pallas kernels, fourier_slots(): pl.pallas_call(functools.partial(fourier_kernel, rows, slots), out_shape=...  33.8 us
    ppermute x7, waiting for transfers between devices, spread(): lax.ppermute(rounded, 'lon', [(i, i ^ distance) for i in range(lon_size)])  25.2 us
    all_to_all x1, waiting for transfers between devices, spread_whole(): return lax.all_to_all(block, 'lon', split_axis=0, concat_axis=0, tiled=True)  25 us
    ppermute x7, starting transfers between devices, spread(): lax.ppermute(rounded, 'lon', [(i, i ^ distance) for i in range(lon_size)])  17.4 us
    all_to_all x2, waiting for transfers between devices, on_device(): lax.all_to_all(chosen, ('lat', 'lon'), split_axis=0, concat_axis=0, tiled...  10.1 us
    all_to_all x2, starting transfers between devices, on_device(): lax.all_to_all(chosen, ('lat', 'lon'), split_axis=0, concat_axis=0, tiled...  6.3 us
    all_to_all x1, starting transfers between devices, spread_whole(): return lax.all_to_all(block, 'lon', split_axis=0, concat_axis=0, tiled=True)  4.84 us
  transfers between devices with their start and end apart: 10, of which 6 were waited for; matrix products, arithmetic and copies ran while one was open for 8% of the time, Pallas kernels for 31%

profile of v5, /device:TPU:0, one launch (start us, length us, event | category | flops | bytes accessed | tf_op | source)
XLA Modules:
  0.0 191.5 jit_solution(7945304971986090743)
XLA Ops:
  0.0 1.1 multiply_convert_fusion.8
  1.1 5.1 %collective-permute-start = (f16[128,1024]{1,0:T(8,128)(2,1)S(1)}, f16[128,1024]{1,0:T(8,128)(2,1)S(1)}, u32[]{:S(2)}, u32[]{:S(2)}) collective-permute-start(f16[128,1024]{1,0:T(8,128)(2,1)S(1)} %bitcast.35), channel_id=1, source_target_pairs={{0,6},{1,7},{2,4},{3,5},{4,2},{5,3},{6,0},{7,1},{8,14},{9,15},{10,... | collective-permute-start | bytes 786440 | tf_op jit(solution)/shard_map/ppermute | solution.py:395
  6.2 2.5 %multiply_convert_fusion.1 = (f16[1,2,64,1024]{3,2,1,0:T(8,128)(2,1)S(1)}, f16[1,2,64,1024]{3,2,1,0:T(8,128)(2,1)S(1)}, f16[1,2,64,1024]{3,2,1,0:T(8,128)(2,1)S(...) fusion(f32[16,2,64,1024]{3,2,1,0:T(8,128)} %param.5, ...), kind=kLoop, calls=%fused_computation.1 | loop fusion | flops 1835008 | bytes 5505052 | tf_op jit(solution)/shard_map/convert_element_type | solution.py:388
  8.7 1.6 collective-permute-start.6
  10.3 0.0 collective-permute-start.5
  10.3 1.7 collective-permute-start.4
  12.0 3.5 %collective-permute-start.3 = (f16[128,1024]{1,0:T(8,128)(2,1)S(1)}, f16[128,1024]{1,0:T(8,128)(2,1)S(1)}, u32[]{:S(2)}, u32[]{:S(2)}) collective-permute-start(f16[128,1024]{1,0:T(8,128)(2,1)S(1)} %bitcast.31), channel_id=1, source_target_pairs={{0,7},{1,6},{2,5},{3,4},{4,3},{5,2},{6,1},{7,0},{8,15},{9,14},{10,... | collective-permute-start | bytes 786440 | tf_op jit(solution)/shard_map/ppermute | solution.py:395
  15.5 0.0 collective-permute-done
  15.5 4.1 %collective-permute-start.2 = (f16[128,1024]{1,0:T(8,128)(2,1)S(1)}, f16[128,1024]{1,0:T(8,128)(2,1)S(1)}, u32[]{:S(2)}, u32[]{:S(2)}) collective-permute-start(f16[128,1024]{1,0:T(8,128)(2,1)S(1)} %bitcast.30), channel_id=1, source_target_pairs={{0,2},{1,3},{2,0},{3,1},{4,6},{5,7},{6,4},{7,5},{8,10},{9,11},{10,... | collective-permute-start | bytes 786440 | tf_op jit(solution)/shard_map/ppermute | solution.py:395
  19.6 4.6 %collective-permute-done.6 = f16[128,1024]{1,0:T(8,128)(2,1)S(1)} collective-permute-done((f16[128,1024]{1,0:T(8,128)(2,1)S(1)}, f16[128,1024]{1,0:T(8,128)(2,1)S(1)}, u32[]{:S(2)}, u32[]{:S(2)}) %collective-permute-start.6) | collective-permute-done | bytes 262176 | tf_op jit(solution)/shard_map/ppermute | solution.py:395
  24.3 0.0 copy-start.2
  24.3 0.7 copy-done.2
  25.0 1.4 collective-permute-start.1
  26.4 4.1 %multiply_convert_fusion = f16[8,2,64,1024]{3,2,1,0:T(8,128)(2,1)} fusion(f32[16,2,64,1024]{3,2,1,0:T(8,128)} %param.5), kind=kLoop, calls=%fused_computation | loop fusion | flops 2097152 | bytes 6291456 | tf_op jit(solution)/shard_map/convert_element_type | solution.py:403
  30.5 0.0 collective-permute-done.5
  30.5 5.6 %collective-permute-done.4 = f16[128,1024]{1,0:T(8,128)(2,1)S(1)} collective-permute-done((f16[128,1024]{1,0:T(8,128)(2,1)S(1)}, f16[128,1024]{1,0:T(8,128)(2,1)S(1)}, u32[]{:S(2)}, u32[]{:S(2)}) %collective-permute-start.4) | collective-permute-done | bytes 262176 | tf_op jit(solution)/shard_map/ppermute | solution.py:395
  36.1 0.0 collective-permute-done.3
  36.1 0.0 collective-permute-done.2
  36.1 0.0 copy-start.3
  36.1 14.9 %collective-permute-done.1 = f16[128,1024]{1,0:T(8,128)(2,1)S(1)} collective-permute-done((f16[128,1024]{1,0:T(8,128)(2,1)S(1)}, f16[128,1024]{1,0:T(8,128)(2,1)S(1)}, u32[]{:S(2)}, u32[]{:S(2)}) %collective-permute-start.1) | collective-permute-done | bytes 262176 | tf_op jit(solution)/shard_map/ppermute | solution.py:395
  51.0 0.0 copy-done.3
  51.0 0.0 copy-start.4
  51.0 0.7 copy-done.4
  51.7 0.0 copy-start.6
  51.7 4.8 %all-to-all-start = ((f16[8,128,1024]{2,1,0:T(8,128)(2,1)}), f16[8,128,1024]{2,1,0:T(8,128)(2,1)S(1)}, u32[]{:S(2)}, u32[]{:S(2)}) async-start(f16[8,128,1024]{2,1,0:T(8,128)(2,1)} %bitcast), calls=%async_computation | async-start | bytes 4194304 | tf_op jit(solution)/shard_map/all_to_all | solution.py:404
  56.6 0.0 copy-start.5
  56.6 0.0 copy-done.6
  56.6 0.6 fusion.1.index_ref
  57.3 1.0 bitcast_dynamic-update-slice_fusion.6
  58.3 1.0 bitcast_dynamic-update-slice_fusion.5
  59.3 0.0 copy-done.5
  59.5 2.5 %stack.42.x_ref = f32[8,128,1024]{2,1,0:T(8,128)} convert(f16[8,128,1024]{2,1,0:T(8,128)(2,1)S(1)} %bitcast_dynamic-update-slice_fusion) | non-fusion elementwise | flops 1048576 | bytes 6291456 | tf_op jit(solution)/shard_map/stack | solution.py:422
  62.1 16.9 %fourier_slots.2 = bf16[4096,128]{1,0:T(8,128)(2,1)} custom-call(s32[2048]{0:T(1024)} %fusion.1.index_ref, s32[1]{0:T(128)} %bitcast.8.me_ref, f32[8,128,1024]{2,1,0:T(8,128)} %stack.42.x_ref, bf16[33,128,256]{2,1,0:T(8,128)(2,1)} %constant.88.clone.high_ref, bf16[33,128,256]{2,1,0:T(8,128)(2,1)} %constant.89.clone.low_ref), custom_call_target="tpu_custom_call" | custom-call | flops 830472192 | bytes 12582912 | tf_op jit(solution)/shard_map/fourier_slots/pallas_call | solution.py:171
  79.0 25.0 %all-to-all-done = f16[8,128,1024]{2,1,0:T(8,128)(2,1)S(1)} async-done(((f16[8,128,1024]{2,1,0:T(8,128)(2,1)}), f16[8,128,1024]{2,1,0:T(8,128)(2,1)S(1)}, u32[]{:S(2)}, u32[]{:S(2)}) %all-to-all-start) | async-done | bytes 2097184 | tf_op jit(solution)/shard_map/all_to_all | solution.py:404
  103.9 3.7 %all-to-all-start.2 = ((bf16[32,128,128]{2,1,0:T(8,128)(2,1)}), bf16[32,128,128]{2,1,0:T(8,128)(2,1)S(1)}, u32[]{:S(2)}, u32[]{:S(2)}) async-start(bf16[32,128,128]{2,1,0:T(8,128)(2,1)} %bitcast.27), calls=%async_computation.2 | async-start | bytes 2097152 | tf_op jit(solution)/shard_map/all_to_all | solution.py:432
  107.6 2.5 %convert_element_type.100.x_ref = f32[8,128,1024]{2,1,0:T(8,128)} convert(f16[8,128,1024]{2,1,0:T(8,128)(2,1)S(1)} %all-to-all-done) | non-fusion elementwise | flops 1048576 | bytes 6291456 | tf_op jit(solution)/shard_map/convert_element_type | solution.py:424
  110.1 16.9 %fourier_slots.3 = bf16[4096,128]{1,0:T(8,128)(2,1)} custom-call(s32[2048]{0:T(1024)} %fusion.1.index_ref, s32[1]{0:T(128)} %constant.81.clone.1.me_ref, f32[8,128,1024]{2,1,0:T(8,128)} %convert_element_type.100.x_ref, bf16[33,128,256]{2,1,0:T(8,128)(2,1)} %constant.88.clone.high_ref, bf16[33,128,256]{2,1,0:T(8,128)(2,1)} %constant.89.clone.low_ref), custom_call_target="tpu_custom_call" | custom-call | flops 830472192 | bytes 12582912 | tf_op jit(solution)/shard_map/fourier_slots/pallas_call | solution.py:171
  127.0 8.1 %all-to-all-done.2.moved_ref = bf16[32,128,128]{2,1,0:T(8,128)(2,1)S(1)} async-done(((bf16[32,128,128]{2,1,0:T(8,128)(2,1)}), bf16[32,128,128]{2,1,0:T(8,128)(2,1)S(1)}, u32[]{:S(2)}, u32[]{:S(2)}) %all-to-all-start.2) | async-done | bytes 1048608 | tf_op jit(solution)/shard_map/all_to_all | solution.py:432
  135.2 0.0 copy-start
  135.2 2.6 %all-to-all-start.1 = ((bf16[32,128,128]{2,1,0:T(8,128)(2,1)}), bf16[32,128,128]{2,1,0:T(8,128)(2,1)S(1)}, u32[]{:S(2)}, u32[]{:S(2)}) async-start(bf16[32,128,128]{2,1,0:T(8,128)(2,1)} %bitcast.26), calls=%async_computation.1 | async-start | bytes 2097152 | tf_op jit(solution)/shard_map/all_to_all | solution.py:432
  137.9 0.6 dynamic-slice_subtract_fusion.limit_ref
  138.4 0.0 copy-done
  138.4 25.0 %legendre_sum.2.refs_0_ = f32[64,2,16,2048]{3,2,1,0:T(8,128)} custom-call(s32[64]{0:T(128)} %dynamic-slice_subtract_fusion.limit_ref, bf16[32,128,128]{2,1,0:T(8,128)(2,1)} %copy-done, bf16[64,2048,256]{2,1,0:T(8,128)(2,1)} %table_ref.3), custom_call_target="tpu_custom_call" | custom-call | flops 1073741824 | bytes 41943040 | tf_op jit(solution)/shard_map/legendre_sum/pallas_call | solution.py:348
  163.5 2.0 %all-to-all-done.1.moved_ref = bf16[32,128,128]{2,1,0:T(8,128)(2,1)S(1)} async-done(((bf16[32,128,128]{2,1,0:T(8,128)(2,1)}), bf16[32,128,128]{2,1,0:T(8,128)(2,1)S(1)}, u32[]{:S(2)}, u32[]{:S(2)}) %all-to-all-start.1) | async-done | bytes 1048608 | tf_op jit(solution)/shard_map/all_to_all | solution.py:432
  165.4 0.0 copy-start.1
  165.4 1.0 copy-done.1
  166.4 25.0 %legendre_sum.3 = f32[64,2,16,2048]{3,2,1,0:T(8,128)} custom-call(s32[64]{0:T(128)} %dynamic-slice_subtract_fusion.limit_ref, bf16[32,128,128]{2,1,0:T(8,128)(2,1)} %copy-done.1, bf16[64,2048,256]{2,1,0:T(8,128)(2,1)} %table_ref.3, f32[64,2,16,2048]{3,2,1,0:T(8,128)} %legendre_sum.2.refs_0_), custom_call_target="tpu_custom_call", output_to_operand_aliasing={{}: (3, {})} | custom-call | flops 1073741824 | bytes 41943040 | tf_op jit(solution)/shard_map/legendre_sum/pallas_call | solution.py:348
  (6 shorter events, 0.3 us)
Async XLA Ops:
  1.1 14.4 %collective-permute-start = (f16[128,1024]{1,0:T(8,128)(2,1)S(1)}, f16[128,1024]{1,0:T(8,128)(2,1)S(1)}, u32[]{:S(2)}, u32[]{:S(2)}) collective-permute-start(f16[128,1024]{1,0:T(8,128)(2,1)S(1)} %bitcast.35), channel_id=1, source_target_pairs={{0,6},{1,7},{2,4},{3,5},{4,2},{5,3},{6,0},{7,1},{8,14},{9,15},{10,... | collective-permute-start | bytes 786440 | tf_op jit(solution)/shard_map/ppermute | solution.py:395
  8.7 15.6 %collective-permute-start.6 = (f16[128,1024]{1,0:T(8,128)(2,1)S(1)}, f16[128,1024]{1,0:T(8,128)(2,1)S(1)}, u32[]{:S(2)}, u32[]{:S(2)}) collective-permute-start(f16[128,1024]{1,0:T(8,128)(2,1)S(1)} %bitcast.34), channel_id=1, source_target_pairs={{0,1},{1,0},{2,3},{3,2},{4,5},{5,4},{6,7},{7,6},{8,9},{9,8},{10,11... | collective-permute-start | bytes 786440 | tf_op jit(solution)/shard_map/ppermute | solution.py:395
  10.3 20.2 %collective-permute-start.5 = (f16[128,1024]{1,0:T(8,128)(2,1)S(1)}, f16[128,1024]{1,0:T(8,128)(2,1)S(1)}, u32[]{:S(2)}, u32[]{:S(2)}) collective-permute-start(f16[128,1024]{1,0:T(8,128)(2,1)S(1)} %bitcast.33), channel_id=1, source_target_pairs={{0,3},{1,2},{2,1},{3,0},{4,7},{5,6},{6,5},{7,4},{8,11},{9,10},{10,... | collective-permute-start | bytes 786440 | tf_op jit(solution)/shard_map/ppermute | solution.py:395
  10.3 25.8 %collective-permute-start.4 = (f16[128,1024]{1,0:T(8,128)(2,1)S(1)}, f16[128,1024]{1,0:T(8,128)(2,1)S(1)}, u32[]{:S(2)}, u32[]{:S(2)}) collective-permute-start(f16[128,1024]{1,0:T(8,128)(2,1)S(1)} %bitcast.32), channel_id=1, source_target_pairs={{0,5},{1,4},{2,7},{3,6},{4,1},{5,0},{6,3},{7,2},{8,13},{9,12},{10,... | collective-permute-start | bytes 786440 | tf_op jit(solution)/shard_map/ppermute | solution.py:395
  12.0 24.1 %collective-permute-start.3 = (f16[128,1024]{1,0:T(8,128)(2,1)S(1)}, f16[128,1024]{1,0:T(8,128)(2,1)S(1)}, u32[]{:S(2)}, u32[]{:S(2)}) collective-permute-start(f16[128,1024]{1,0:T(8,128)(2,1)S(1)} %bitcast.31), channel_id=1, source_target_pairs={{0,7},{1,6},{2,5},{3,4},{4,3},{5,2},{6,1},{7,0},{8,15},{9,14},{10,... | collective-permute-start | bytes 786440 | tf_op jit(solution)/shard_map/ppermute | solution.py:395
  15.5 20.6 %collective-permute-start.2 = (f16[128,1024]{1,0:T(8,128)(2,1)S(1)}, f16[128,1024]{1,0:T(8,128)(2,1)S(1)}, u32[]{:S(2)}, u32[]{:S(2)}) collective-permute-start(f16[128,1024]{1,0:T(8,128)(2,1)S(1)} %bitcast.30), channel_id=1, source_target_pairs={{0,2},{1,3},{2,0},{3,1},{4,6},{5,7},{6,4},{7,5},{8,10},{9,11},{10,... | collective-permute-start | bytes 786440 | tf_op jit(solution)/shard_map/ppermute | solution.py:395
  24.3 0.7 copy-start.2
  25.0 26.0 %collective-permute-start.1 = (f16[128,1024]{1,0:T(8,128)(2,1)S(1)}, f16[128,1024]{1,0:T(8,128)(2,1)S(1)}, u32[]{:S(2)}, u32[]{:S(2)}) collective-permute-start(f16[128,1024]{1,0:T(8,128)(2,1)S(1)} %bitcast.29), channel_id=1, source_target_pairs={{0,4},{1,5},{2,6},{3,7},{4,0},{5,1},{6,2},{7,3},{8,12},{9,13},{10,... | collective-permute-start | bytes 786440 | tf_op jit(solution)/shard_map/ppermute | solution.py:395
  36.1 14.9 %copy-start.3 = (f16[128,1024]{1,0:T(8,128)(2,1)}, f16[128,1024]{1,0:T(8,128)(2,1)S(1)}, u32[]{:S(2)}) copy-start(f16[128,1024]{1,0:T(8,128)(2,1)S(1)} %collective-permute-done.2) | copy-start | bytes 786436
  51.0 0.7 copy-start.4
  51.7 4.9 %copy-start.6 = (s32[2048]{0:T(1024)S(1)}, s32[2048]{0:T(1024)}, u32[]{:S(2)}) copy-start(s32[2048]{0:T(1024)} %param.7) | copy-start | bytes 24580
  51.7 52.2 %all-to-all-start = ((f16[8,128,1024]{2,1,0:T(8,128)(2,1)}), f16[8,128,1024]{2,1,0:T(8,128)(2,1)S(1)}, u32[]{:S(2)}, u32[]{:S(2)}) async-start(f16[8,128,1024]{2,1,0:T(8,128)(2,1)} %bitcast), calls=%async_computation | async-start | bytes 4194304 | tf_op jit(solution)/shard_map/all_to_all | solution.py:404
  56.6 2.7 %copy-start.5 = (f16[128,1024]{1,0:T(8,128)(2,1)S(1)}, f16[128,1024]{1,0:T(8,128)(2,1)}, u32[]{:S(2)}) copy-start(f16[128,1024]{1,0:T(8,128)(2,1)} %copy-done.4) | copy-start | bytes 786436
  103.9 31.2 %all-to-all-start.2 = ((bf16[32,128,128]{2,1,0:T(8,128)(2,1)}), bf16[32,128,128]{2,1,0:T(8,128)(2,1)S(1)}, u32[]{:S(2)}, u32[]{:S(2)}) async-start(bf16[32,128,128]{2,1,0:T(8,128)(2,1)} %bitcast.27), calls=%async_computation.2 | async-start | bytes 2097152 | tf_op jit(solution)/shard_map/all_to_all | solution.py:432
  135.2 3.2 %copy-start = (bf16[32,128,128]{2,1,0:T(8,128)(2,1)}, bf16[32,128,128]{2,1,0:T(8,128)(2,1)S(1)}, u32[]{:S(2)}) copy-start(bf16[32,128,128]{2,1,0:T(8,128)(2,1)S(1)} %all-to-all-done.2.moved_ref) | copy-start | bytes 3145732
  135.2 30.2 %all-to-all-start.1 = ((bf16[32,128,128]{2,1,0:T(8,128)(2,1)}), bf16[32,128,128]{2,1,0:T(8,128)(2,1)S(1)}, u32[]{:S(2)}, u32[]{:S(2)}) async-start(bf16[32,128,128]{2,1,0:T(8,128)(2,1)} %bitcast.26), calls=%async_computation.1 | async-start | bytes 2097152 | tf_op jit(solution)/shard_map/all_to_all | solution.py:432
  165.4 1.0 copy-start.1
